TPU v7x, 32 devices: a whole 2x2x4 slice. The times are simulated.
32 devices in a mesh: dp: 4 (over y, x), blk: 4 (over z), head: 2 (over core).
Axes of the slice: x: 2, y: 2, z: 4, core: 2. Of those that a mesh axis runs over, the one named last changes fastest.
Arguments:
- tokens: bfloat16 [4, 2048, 768], P('dp', ('blk', 'head')), may hold values from -6 to 6
- segment: int32 [4, 2048], P('dp'), may hold values from 0 to 7, as said below
- w_qkv: bfloat16 [768, 2304], P(('dp', 'blk', 'head')), may hold values from -0.21875 to 0.21875
- bias_query: bfloat16 [768], P(('dp', 'blk', 'head')), may hold values from -3 to 3
- bias_value: bfloat16 [768], P(('dp', 'blk', 'head')), may hold values from -3 to 3
- w_out: bfloat16 [768, 768], P(('dp', 'blk', 'head')), may hold values from -1.75 to 1.75
- bias_out: bfloat16 [768], P(('dp', 'blk', 'head')), may hold values from -3 to 3
- gain_attn: bfloat16 [768], P(('dp', 'blk', 'head')), may hold values from 0.099609375 to 1.8984375
- shift_attn: bfloat16 [768], P(('dp', 'blk', 'head')), may hold values from -3 to 3
- w_in: bfloat16 [768, 3072], P(('dp', 'blk', 'head')), may hold values from -0.21875 to 0.21875
- bias_in: bfloat16 [3072], P(('dp', 'blk', 'head')), may hold values from -3 to 3
- w_down: bfloat16 [3072, 768], P(('dp', 'blk', 'head')), may hold values from -0.109375 to 0.109375
- bias_down: bfloat16 [768], P(('dp', 'blk', 'head')), may hold values from -3 to 3
- gain_ffn: bfloat16 [768], P(('dp', 'blk', 'head')), may hold values from 0.099609375 to 1.8984375
- shift_ffn: bfloat16 [768], P(('dp', 'blk', 'head')), may hold values from -3 to 3
- cotangent: bfloat16 [4, 2048, 768], P('dp', ('blk', 'head')), may hold values from -6 to 6
Outputs:
- output: bfloat16 [4, 2048, 768], P('dp', ('blk', 'head'))
- grad_tokens: float32 [4, 2048, 768], P('dp', ('blk', 'head'))
- grad_w_qkv: float32 [768, 2304], P(('dp', 'blk', 'head'))
- grad_bias_query: float32 [768], P(('dp', 'blk', 'head'))
- grad_bias_value: float32 [768], P(('dp', 'blk', 'head'))
- grad_w_out: float32 [768, 768], P(('dp', 'blk', 'head'))
- grad_bias_out: float32 [768], P(('dp', 'blk', 'head'))
- grad_gain_attn: float32 [768], P(('dp', 'blk', 'head'))
- grad_shift_attn: float32 [768], P(('dp', 'blk', 'head'))
- grad_w_in: float32 [768, 3072], P(('dp', 'blk', 'head'))
- grad_bias_in: float32 [3072], P(('dp', 'blk', 'head'))
- grad_w_down: float32 [3072, 768], P(('dp', 'blk', 'head'))
- grad_bias_down: float32 [768], P(('dp', 'blk', 'head'))
- grad_gain_ffn: float32 [768], P(('dp', 'blk', 'head'))
- grad_shift_ffn: float32 [768], P(('dp', 'blk', 'head'))
Inputs may be any that keep to these rules, and one draw needn't show every extreme that they name: `segment`: document ids of the tokens of each sequence; ids never fall along a sequence (each document is one contiguous run of tokens), and every id of 0 to 7 occurs in every sequence. Among the 1 sequence of each index of dp, one (drawn from the seed) holds a document that covers tokens of the first and of the last of its 4 token blocks.
All inputs are finite; a program needn't handle non-finite values.
Results may differ from a plain program's by a relative error of at most 0.023.
Values may be sent and summed in bfloat16 or wider, within the bound.
A program may use at most 192 MiB of HBM per device.

v0:
```python
import functools

import jax
import jax.numpy as jnp
from jax import lax
from jax.experimental import pallas as pl
from jax.experimental.pallas import tpu as pltpu
from jax.sharding import PartitionSpec as P

MESH = pl.DeviceIdType.MESH
F32, BF16 = jnp.float32, jnp.bfloat16
HD = 64
HEADS = 12
BIG = 2.0**30

class Net:
    def __init__(self, nd, nb, nc):
        self.nd, self.nb, self.nc = nd, nb, nc
        self.levels = nd.bit_length() - 1
        self.d, self.b, self.c = (lax.axis_index(a) for a in ("dp", "blk", "head"))
        top = self.levels - 1
        self.stride = [(1 - self.c) * 2**k + self.c * 2 ** (top - k) for k in range(self.levels)]
        self.sibling = (self.d, self.b, self.nc - 1 - self.c)
        steps = [s * (1 - 2 * ((self.d // s) % 2)) for s in self.stride]
        self.flipped = [self.d]
        for step in steps:
            self.flipped += [d + step for d in self.flipped]
        self.nearest = [self.find_near(e) for e in range(self.nb)]

    def flips(self, mask):
        return self.flipped[mask]

    def across(self, k):
        return (self.flipped[1 << k], self.b, self.c)

    def near(self, e):
        return self.nearest[e]

    def find_near(self, e):
        order = [sorted(range(self.nb), key=lambda j: (abs(j - i), -j)) for i in range(self.nb)]
        got = order[0][e]
        for i in range(1, self.nb):
            got = jnp.where(self.b == i, order[i][e], got)
        return got

    def near_at(self, e):
        got = self.near(0)
        for i in range(1, self.nb):
            got = jnp.where(e == i, self.near(i), got)
        return got

    def slot(self, mask, blk):
        return (self.flips(mask) * self.nb + blk) * self.nc + self.c

    def peers(self):
        out = [(self.d, (self.b + u) % self.nb, self.c) for u in range(1, self.nb)]
        out += [self.across(k) for k in range(self.levels)]
        return out + [self.sibling]

    def barrier(self):
        bar = pltpu.get_barrier_semaphore()
        ps = self.peers()
        for p in ps:
            pl.semaphore_signal(bar, inc=1, device_id=p, device_id_type=MESH)
        pl.semaphore_wait(bar, len(ps))


def remote(src, dst, send, recv, dev):
    return pltpu.make_async_remote_copy(src_ref=src, dst_ref=dst, send_sem=send, recv_sem=recv, device_id=dev, device_id_type=MESH)


def blocks_of(full):
    return (lambda i: full.at[i]), (lambda k: full.at[pl.ds(0, k)])


def rows_of(full, rows, offset=0, stride=None):
    every = rows if stride is None else stride

    def place(i):
        return full.at[pl.ds(pl.multiple_of(i * every + offset, 8), rows)]

    return place, (lambda k: full.at[pl.ds(0, k * rows)])


class Gather:
    def __init__(self, net, mine, place, span, sems, narrow=False, direct=False):
        self.net, self.mine, self.place, self.span, self.narrow, self.direct = net, mine, place, span, narrow, direct
        self.zsend, self.xsend, self.ssend, self.srecv, self.recv = sems

    def at(self, mask, blk):
        n = self.net
        if self.narrow:
            return self.place(blk * n.nc + n.c)
        return self.place(n.slot(mask, blk))

    def rsem(self, mask, blk):
        return self.recv.at[mask * self.net.nb + blk]

    def spread(self, mask, blk, src, dst):
        n = self.net
        if not self.narrow:
            for k in range(n.levels):
                if mask < (1 << k):
                    remote(src, dst, self.xsend, self.rsem(mask + (1 << k), blk), n.across(k)).start()
        arrival = self.srecv.at[blk] if self.narrow else self.srecv
        remote(src, dst, self.ssend, arrival, n.sibling).start()

    def along(self, blk, src, dst):
        n = self.net
        sem = self.rsem(0, blk)

        @pl.when((n.b < n.nb - 1) & (blk <= n.b))
        def _():
            remote(src, dst, self.zsend, sem, (n.d, n.b + 1, n.c)).start()

        @pl.when((n.b > 0) & (blk >= n.b))
        def _():
            remote(src, dst, self.zsend, sem, (n.d, n.b - 1, n.c)).start()

    def own_line(self):
        n = self.net
        dst = self.at(0, n.b)
        if not self.direct:
            self.along(n.b, self.mine, dst)
            return
        for e in range(n.nb - 1, 0, -1):
            remote(self.mine, dst, self.zsend, self.rsem(0, n.b), (n.d, n.near(e), n.c)).start()

    def own_spread(self):
        self.spread(0, self.net.b, self.mine, self.at(0, self.net.b))

    def z(self, e):
        blk = self.net.near(e)
        dst = self.at(0, blk)
        pltpu.make_async_copy(dst, dst, self.rsem(0, blk)).wait()
        if not self.direct:
            self.along(blk, dst, dst)
        self.spread(0, blk, dst, dst)

    def x(self, mask, e):
        n = self.net
        blk = n.near(e)
        dst = self.at(mask, blk)
        pltpu.make_async_copy(dst, dst, self.rsem(mask, blk)).wait()
        self.spread(mask, blk, dst, dst)

    def own(self, sem):
        n = self.net
        return pltpu.make_async_copy(self.mine, self.at(0, n.b), sem)

    def wait_sibling_block(self, blk):
        one = self.span(1)
        pltpu.make_async_copy(one, one, self.srecv.at[blk]).wait()

    def wait_sibling(self):
        n = self.net
        if self.narrow:
            for blk in range(n.nb):
                self.wait_sibling_block(blk)
            return
        half = self.span(n.nd * n.nb)
        pltpu.make_async_copy(half, half, self.srecv).wait()

    def drain(self):
        n = self.net
        half = self.span(n.nb if self.narrow else n.nd * n.nb)
        pltpu.make_async_copy(half, half, self.ssend).wait()
        if not self.narrow:
            part = self.span((n.nd - 1) * n.nb)
            pltpu.make_async_copy(part, part, self.xsend).wait()
        if self.direct:
            sent = self.span(n.nb - 1)
            pltpu.make_async_copy(sent, sent, self.zsend).wait()
            return
        edge = (n.b == 0) | (n.b == n.nb - 1)

        @pl.when(edge)
        def _():
            one = self.span(1)
            pltpu.make_async_copy(one, one, self.zsend).wait()

        @pl.when(jnp.logical_not(edge))
        def _():
            many = self.span(n.nb + 1)
            pltpu.make_async_copy(many, many, self.zsend).wait()


def gather_refs(four, recv, block, p, narrow):
    last = block.at[p] if narrow else four.at[p, 3]
    return [four.at[p, 0], four.at[p, 1], four.at[p, 2], last, recv.at[p]]


def gather_sems(n_pieces, nd, nb):
    return [pltpu.SemaphoreType.DMA((n_pieces, 4)), pltpu.SemaphoreType.DMA((n_pieces, nd * nb)), pltpu.SemaphoreType.DMA]


class Scatter:
    def __init__(self, net, parts, place, theirs, landing, span, xrecv, zrecv, out, sems, narrow=False, extra=(), early=False, direct=False):
        self.net, self.parts, self.place, self.theirs, self.landing = net, parts, place, theirs, landing
        self.span, self.xbuf, self.zbuf, self.out, self.extra = span, xrecv, zrecv, out, extra
        self.sib_send, self.x_send, self.z_send, self.sib_sem, self.x_sem, self.z_sem = sems
        self.narrow, self.seen, self.early, self.direct = narrow, set(), early, direct
        self.nd = 1 if narrow else net.nd
        self.levels = 0 if narrow else net.levels

    def home(self, mask):
        return 0 if self.narrow else self.net.flips(mask)

    def start(self):
        for mask in range(self.nd - 1, -1, -1):
            self.start_home(self.home(mask))

    def start_home(self, d):
        for blk in range(self.net.nb):
            self.send(d * self.net.nb + blk, d)

    def send(self, at, sem):
        remote(self.theirs(at), self.landing(at), self.sib_send, self.sib_sem.at[sem], self.net.sibling).start()

    def arrived(self, sem, count):
        some = self.span(count)
        pltpu.make_async_copy(some, some, self.sib_sem.at[sem]).wait()

    def sent(self):
        some = self.span(self.nd * self.net.nb)
        pltpu.make_async_copy(some, some, self.sib_send).wait()

    def x_at(self, k, mask, blk):
        return ((1 << k) - 1 + mask) * self.net.nb + blk

    def z_at(self, side, blk, owner):
        return blk + side * jnp.where(blk == owner, self.net.nb - blk, 0)

    def add(self, at, more, to, extra=()):
        for pick, places in self.parts(at):
            def chosen(ref):
                return ref if pick is None else ref.at[pick]

            add_up(places + [chosen(m) for m in more] + list(extra), chosen(to))

    def reduce(self, mask, e):
        n = self.net
        blk = n.near(e)
        if self.narrow:
            self.arrived(blk, 1)
        elif mask not in self.seen:
            self.seen.add(mask)
            self.arrived(self.home(mask), n.nb)
        at = self.home(mask) * n.nb + blk
        place = self.place(at)
        more = []
        for k in range(self.levels - 1, -1, -1):
            if mask < (1 << k):
                i = self.x_at(k, mask, blk)
                got = self.xbuf.at[i]
                pltpu.make_async_copy(got, got, self.x_sem.at[i]).wait()
                more.append(got)
        if mask:
            k = mask.bit_length() - 1
            self.add(at, more, place)
            i = self.x_at(k, mask - (1 << k), blk)
            remote(place, self.xbuf.at[i], self.x_send, self.x_sem.at[i], n.across(k)).start()
            return

        if self.direct:
            if e:
                self.add(at, more, place)
                remote(place, self.zbuf.at[n.b], self.z_send, self.z_sem.at[n.b], (n.d, blk, n.c)).start()
                return
            for u in range(1, n.nb):
                got = self.zbuf.at[n.near(u)]
                pltpu.make_async_copy(got, got, self.z_sem.at[n.near(u)]).wait()
                more.append(got)
            self.add(at, more, self.out, self.extra)
            return

        def line(side, there):
            i = self.z_at(side, blk, n.b)
            got = self.zbuf.at[i]

            @pl.when(there)
            def _():
                pltpu.make_async_copy(got, got, self.z_sem.at[i]).wait()

            more.append(got)

        if e == 0:
            line(0, n.b > 0)
            line(1, n.b < n.nb - 1)
            self.add(at, more, self.out, self.extra)
            return
        side = jnp.where(blk > n.b, 0, 1)
        line(side, jnp.where(blk > n.b, n.b, n.nb - 1 - n.b) > 0)
        self.add(at, more, place)
        to = n.b + 1 - 2 * side
        i = self.z_at(side, blk, to)
        remote(place, self.zbuf.at[i], self.z_send, self.z_sem.at[i], (n.d, to, n.c)).start()

    def clear_edges(self):
        n = self.net
        if self.direct:
            return

        def clear(i, carry):
            self.zbuf[i] = jnp.zeros(self.zbuf.shape[1:], self.zbuf.dtype)
            return carry

        @pl.when(n.b == 0)
        def _():
            lax.fori_loop(0, n.nb, clear, 0)

        @pl.when(n.b == n.nb - 1)
        def _():
            lax.fori_loop(0, n.nb - 1, clear, 0)
            clear(n.nb, 0)

    def drain(self):
        n = self.net
        if not self.early:
            self.sent()
        if not self.narrow:
            some = self.xbuf.at[pl.ds(0, (n.nd - 1) * n.nb)]
            pltpu.make_async_copy(some, some, self.x_send).wait()
        some = self.zbuf.at[pl.ds(0, n.nb - 1)]
        pltpu.make_async_copy(some, some, self.z_send).wait()


def add_up(terms, to):
    shape = to.shape
    rows = shape[-2]
    step = rows
    while step % 2 == 0 and step > 32:
        step //= 2
    lead = [()] if len(shape) == 2 else [(g,) for g in range(shape[0])]
    for g in lead:
        for r in range(0, rows, step):
            at = g + (slice(r, r + step),)
            total = terms[0][at].astype(F32)
            for t in terms[1:]:
                total = total + t[at].astype(F32)
            to[at] = total.astype(to.dtype)


class AllSum:
    def __init__(self, net, value, got, send, recv):
        self.net, self.value, self.got, self.send, self.recv = net, value, got, send, recv

    def copy(self, stage, dev, src, slot):
        return remote(self.value.at[src], self.got.at[slot], self.send.at[slot], self.recv.at[slot], dev)

    def stages(self):
        n = self.net
        devs = [n.sibling] + [n.across(k) for k in range(n.levels)]
        steps = []
        for i, dev in enumerate(devs):
            steps.append(functools.partial(self.one, i, dev))
        steps.append(self.line_start)
        steps.append(self.line_end)
        return [lambda: self.copy(0, devs[0], 0, 0).start()] + steps

    def one(self, i, dev):
        n = self.net
        self.copy(i, dev, i, i).wait()
        self.value[i + 1] = self.value[i] + self.got[i]
        if i + 1 <= n.levels:
            self.copy(i + 1, n.across(i), i + 1, i + 1).start()

    def line_copy(self, u):
        n = self.net
        return self.copy(None, (n.d, (n.b + u) % n.nb, n.c), n.levels + 1, n.levels + u)

    def line_start(self):
        for u in range(1, self.net.nb):
            self.line_copy(u).start()

    def line_end(self):
        n = self.net
        for u in range(1, n.nb):
            self.line_copy(u).wait()
        total = self.value[n.levels + 1]
        for u in range(1, n.nb):
            total = total + self.got[n.levels + u]
        self.value[0] = total


def scatter_sems(n_pieces, nd, nb):
    return [
        pltpu.SemaphoreType.DMA((n_pieces, 3)),
        pltpu.SemaphoreType.DMA((n_pieces, max(nd, nb))),
        pltpu.SemaphoreType.DMA((n_pieces, (nd - 1) * nb)),
        pltpu.SemaphoreType.DMA((n_pieces, nb + 1)),
    ]


def dot(a, b, dims=((1,), (0,))):
    return lax.dot_general(a, b, (dims, ((), ())), preferred_element_type=F32)


def mask_lanes(seg_row, count):
    lanes = lax.broadcasted_iota(jnp.int32, (128, count), 0)
    return jnp.transpose(jnp.where(lanes == seg_row, -1.0, 0.0).astype(F32), (1, 0))


def project_keys(i, step, tok, wk, wv, bias_v, seg, kaug, v_scr):
    at = pl.ds(pl.multiple_of(i * step, step), step)
    piece = tok[at, :]
    keys = dot(piece, wk).astype(BF16)
    vals = (dot(piece, wv) + bias_v).astype(BF16)
    lanes = mask_lanes(seg[:, at], step).astype(BF16)
    for p in range(kaug.shape[0]):
        kaug[p, at, 0:128] = keys[:, p * 128:(p + 1) * 128]
        kaug[p, at, 128:256] = lanes
        v_scr[p, at, :] = vals[:, p * 128:(p + 1) * 128]


def project_queries(tok, wq, bias_q, seg, qaug, blk, qlen):
    mine = pl.ds(pl.multiple_of(blk * qlen, qlen), qlen)
    query = (dot(tok[mine, :], wq) + bias_q).astype(BF16)
    lane = lax.broadcasted_iota(jnp.int32, (qlen, 128), 1)
    feat = jnp.where(lane < 8, BIG * (1.0 + mask_lanes(seg[:, mine], qlen)), 0.0).astype(BF16)
    for p in range(qaug.shape[0] // 2):
        q_pair = query[:, p * 128:(p + 1) * 128].astype(F32) * HD**-0.5
        for half in range(2):
            keep = (lane >= 64) if half else (lane < 64)
            qaug[2 * p + half, :, 0:128] = jnp.where(keep, q_pair, 0.0).astype(BF16)
            qaug[2 * p + half, :, 128:256] = feat


def attend_chunk(i, qaug, kaug, v_scr, o_scr, exact_scr, lse_scr, chunk, per_head):
    h = i // per_head
    at = pl.ds(pl.multiple_of((i % per_head) * chunk, chunk), chunk)
    s = dot(qaug[h, at, :], kaug[h // 2], ((1,), (1,)))
    top = jnp.max(s, axis=-1, keepdims=True)
    p = jnp.exp(s - top)
    total = jnp.sum(p, axis=-1, keepdims=True)
    low = p.astype(BF16)
    rest = (p - low.astype(F32)).astype(BF16)
    value = v_scr[h // 2]
    o = dot(low, value)
    inverse = 1.0 / total
    o_scr[h, at, :] = o * inverse
    exact_scr[h, at, :] = (o + dot(rest, value)) * inverse
    lse_scr[h, at, :] = jnp.broadcast_to(top + jnp.log(total), (chunk, 128))


def attend_block(h, at, qaug, kaug, v_scr, top_scr, sum_scr, o_scr, rest_scr):
    s = dot(qaug[h], kaug[h // 2, at, :], ((1,), (1,)))
    before = top_scr[h]
    top = jnp.maximum(before, jnp.broadcast_to(jnp.max(s, axis=-1, keepdims=True), before.shape))
    p = jnp.exp(s - jnp.concatenate([top] * (s.shape[1] // 128), axis=1))
    fade = jnp.exp(before - top)
    low = p.astype(BF16)
    rest = (p - low.astype(F32)).astype(BF16)
    value = v_scr[h // 2, at, :]
    top_scr[h] = top
    sum_scr[h] = sum_scr[h] * fade + jnp.broadcast_to(jnp.sum(p, axis=-1, keepdims=True), before.shape)
    o_scr[h] = o_scr[h] * fade + dot(low, value)
    rest_scr[h] = rest_scr[h] * fade + dot(rest, value)


def close_blocks(top_scr, sum_scr, o_scr, rest_scr):
    for h in range(o_scr.shape[0]):
        total = sum_scr[h]
        inverse = 1.0 / total
        o = o_scr[h]
        rest_scr[h] = (o + rest_scr[h]) * inverse
        o_scr[h] = o * inverse
        top_scr[h] = top_scr[h] + jnp.log(total)


def join_heads(scr, p, at=slice(None)):
    first, second = scr[2 * p, at, :], scr[2 * p + 1, at, :]
    lane = lax.broadcasted_iota(jnp.int32, first.shape, 1)
    return jnp.where(lane < 64, first, second)


def head_columns(w, part, c, width):
    return w[:, pl.ds(pl.multiple_of((part * 2 + c) * width, 128), width)]


def fwd_kernel(tok, w, bias, seg, ctx, kaug, v_scr, qaug, lse_out, exact, lse_scr, o_scr, exact_scr, chunk=256):
    blk, c = lax.axis_index("blk"), lax.axis_index("head")
    qlen, width = ctx.shape
    total = tok.shape[0]
    step = min(512, total)
    wk, wv = head_columns(w, 1, c, width), head_columns(w, 2, c, width)

    def rows(i, carry):
        project_keys(i, step, tok, wk, wv, bias[1:2, :], seg, kaug, v_scr)
        return carry

    lax.fori_loop(0, total // step, rows, 0)
    project_queries(tok, head_columns(w, 0, c, width), bias[0:1, :], seg, qaug, blk, qlen)
    per_head = qlen // chunk

    def go(i, carry):
        attend_chunk(i, qaug, kaug, v_scr, o_scr, exact_scr, lse_scr, chunk, per_head)
        return carry

    lax.fori_loop(0, (width // HD) * per_head, go, 0)
    finish_forward(o_scr, exact_scr, lse_scr, lambda p, v: store_lanes(ctx, p, v), lse_out, exact)


def store_lanes(ref, p, value):
    ref[:, p * 128:(p + 1) * 128] = value


def finish_forward(o_scr, exact_scr, lse_scr, put, lse_out, exact):
    for p in range(o_scr.shape[0] // 2):
        put(p, join_heads(o_scr, p).astype(BF16))
        exact[p] = join_heads(exact_scr, p)
    for h in range(o_scr.shape[0]):
        lse_out[h] = jnp.transpose(lse_scr[h], (1, 0))[0:8, :]


def prepare_backward(gctx_of, exact, do_m, delta_row):
    pairs, qlen, _ = exact.shape
    lane = lax.broadcasted_iota(jnp.int32, (qlen, 128), 1)
    for p in range(pairs):
        grad = gctx_of(p)
        product = grad.astype(F32) * exact[p]
        for half in range(2):
            keep = (lane >= 64) if half else (lane < 64)
            do_m[2 * p + half] = jnp.where(keep, grad, jnp.zeros_like(grad))
            across = jnp.transpose(jnp.where(keep, product, 0.0), (1, 0))
            delta_row[2 * p + half] = jnp.broadcast_to(jnp.sum(across, axis=0, keepdims=True), (8, qlen))


def bwd_pair(pair, qaug, k_part, v_part, do_m, lse_row, delta_row, dq_scr, put, first, qs=slice(None)):
    dk = dv = None
    for half in range(2):
        h = 2 * pair + half
        q_part, do_part = qaug[h, qs, :], do_m[h, qs, :]
        s = dot(k_part, q_part, ((1,), (1,)))
        p = jnp.exp(s - lse_row[h, 0:1, qs])
        dp = dot(v_part, do_part, ((1,), (1,)))
        ds = (p * (dp - delta_row[h, 0:1, qs])).astype(BF16)
        v_term = dot(p.astype(BF16), do_part)
        k_term = dot(ds, q_part[:, 0:128])
        dv = v_term if dv is None else dv + v_term
        dk = k_term if dk is None else dk + k_term
        dq = dot(k_part[:, 0:128], ds, ((0,), (0,)))
        if first is True:
            dq_scr[h, :, qs] = dq
        elif first is None:
            dq_scr[h, :, qs] += dq
        else:
            dq_scr[h, :, qs] = jnp.where(first, dq, dq_scr[h, :, qs] + dq)
    put(dk, dv)


def join_dq(dq_scr, p):
    qlen = dq_scr.shape[2]
    lane = lax.broadcasted_iota(jnp.int32, (qlen, 128), 1)
    first, second = jnp.transpose(dq_scr[2 * p], (1, 0)), jnp.transpose(dq_scr[2 * p + 1], (1, 0))
    return (jnp.where(lane < 64, first, second) * HD**-0.5).astype(BF16)


VMEM = pl.BlockSpec(memory_space=pltpu.VMEM)
HBM = pl.BlockSpec(memory_space=pltpu.HBM)


def params(limit, collective=None):
    more = {} if collective is None else dict(collective_id=collective, has_side_effects=True)
    return pltpu.CompilerParams(vmem_limit_bytes=limit << 20, **more)


def lane_mean(x):
    return jnp.mean(x, axis=-1, keepdims=True)


def norm_parts(hidden):
    centered = hidden - lane_mean(hidden)
    scale = lax.rsqrt(lane_mean(centered * centered) + 1e-12)
    return centered * scale, scale


def norm_back(grad, unit, scale, gain):
    scaled = grad * gain
    return scale * (scaled - lane_mean(scaled) - unit * lane_mean(scaled * unit))


def gelu_and_slope(pre):
    cdf = 0.5 * (1.0 + lax.erf(pre * 0.7071067811865476))
    return pre * cdf, cdf + pre * (0.3989422804014327 * jnp.exp(-0.5 * pre * pre))


def column_sum(x):
    return jnp.sum(x, axis=0, keepdims=True)


def ffn_kernel(
    ctx, tok, cot, vecs, bias_in, w_out_h, w_in_h, w_down_h,
    out, resid_grad, gctx, dw_down_h, dw_in_h, dw_out_h, sums,
    w_out, w_in, w_down, act, slope, dw_a, dw_b, dw_c, in_sem, out_sem,
):
    groups, rows, half = ctx.shape
    width, ff = w_in.shape
    step = width
    loads = [
        pltpu.make_async_copy(src, dst, in_sem.at[i])
        for i, (src, dst) in enumerate([(w_out_h, w_out), (w_in_h, w_in), (w_down_h, w_down)])
    ]
    for load in loads:
        load.start()
    bias_out, gain_one, shift_one = vecs[2:3, :], vecs[3:4, :], vecs[4:5, :]
    bias_down, gain_two, shift_two = vecs[5:6, :], vecs[6:7, :], vecs[7:8, :]
    context = jnp.concatenate([ctx[g] for g in range(groups)], axis=1)
    loads[0].wait()
    resid_one = tok[...].astype(F32) + (dot(context, w_out[...]) + bias_out)
    unit_one, scale_one = norm_parts(resid_one)
    normed = unit_one * gain_one + shift_one
    normed_low = normed.astype(BF16)
    loads[1].wait()
    chunks = [slice(i, i + step) for i in range(0, ff, step)]
    for at in chunks:
        pre = dot(normed_low, w_in[:, at]) + bias_in[0:1, at]
        value, grad = gelu_and_slope(pre)
        act[:, at] = value.astype(BF16)
        slope[:, at] = grad
    loads[2].wait()
    resid_two = normed + (dot(act[...], w_down[...]) + bias_down)
    unit_two, scale_two = norm_parts(resid_two)
    out[...] = (unit_two * gain_two + shift_two).astype(BF16)
    grad_out = cot[...].astype(F32)
    grad_two = norm_back(grad_out, unit_two, scale_two, gain_two)
    grad_ffn = grad_two.astype(BF16)
    sums[0:2, :] = jnp.zeros((2, width), F32)
    sums[5:6, :] = column_sum(grad_ffn.astype(F32))
    sums[6:7, :] = column_sum(grad_out * unit_two)
    sums[7:8, :] = column_sum(grad_out)
    stores = []

    def store(src, dst):
        copy = pltpu.make_async_copy(src, dst, out_sem.at[len(stores)])
        copy.start()
        stores.append(copy)

    for at in chunks:
        dw_a[at, :] = dot(act[:, at], grad_ffn, ((0,), (0,))).astype(BF16)
        store(dw_a.at[at], dw_down_h.at[at])
    grad_normed = grad_two
    for i, at in enumerate(chunks):
        grad_act = dot(grad_ffn, w_down[at, :], ((1,), (1,)))
        grad_pre = (grad_act * slope[:, at]).astype(BF16)
        sums[8 + i:9 + i, :] = column_sum(grad_pre.astype(F32))
        dw_b[:, at] = dot(normed_low, grad_pre, ((0,), (0,))).astype(BF16)
        grad_normed = grad_normed + dot(grad_pre, w_in[:, at], ((1,), (1,)))
    store(dw_b, dw_in_h)
    sums[8 + len(chunks):, :] = jnp.zeros((sums.shape[0] - 8 - len(chunks), width), F32)
    sums[3:4, :] = column_sum(grad_normed * unit_one)
    sums[4:5, :] = column_sum(grad_normed)
    grad_one = norm_back(grad_normed, unit_one, scale_one, gain_one)
    resid_grad[...] = grad_one
    grad_attn = grad_one.astype(BF16)
    sums[2:3, :] = column_sum(grad_attn.astype(F32))
    dw_c[...] = dot(context, grad_attn, ((0,), (0,))).astype(BF16)
    store(dw_c, dw_out_h)
    grad_context = dot(grad_attn, w_out[...], ((1,), (1,))).astype(BF16)
    for g in range(groups):
        gctx[g] = grad_context[:, g * half:(g + 1) * half]
    for copy in stores:
        copy.wait()


def feed_forward(ctx, tok, cot, vecs, bias_in, w_out, w_in, w_down):
    groups, rows, half = ctx.shape
    width, ff = w_in.shape
    n_sums = 8 + -(-(ff // width) // 8) * 8
    return pl.pallas_call(
        ffn_kernel,
        out_shape=[
            jax.ShapeDtypeStruct((rows, width), BF16),
            jax.ShapeDtypeStruct((rows, width), F32),
            jax.ShapeDtypeStruct((groups, rows, half), BF16),
            jax.ShapeDtypeStruct((ff, width), BF16),
            jax.ShapeDtypeStruct((width, ff), BF16),
            jax.ShapeDtypeStruct((width, width), BF16),
            jax.ShapeDtypeStruct((n_sums, width), F32),
        ],
        in_specs=[VMEM] * 5 + [HBM] * 3,
        out_specs=[VMEM] * 3 + [HBM] * 3 + [VMEM],
        scratch_shapes=[
            pltpu.VMEM((width, width), BF16),
            pltpu.VMEM((width, ff), BF16),
            pltpu.VMEM((ff, width), BF16),
            pltpu.VMEM((rows, ff), BF16),
            pltpu.VMEM((rows, ff), F32),
            pltpu.VMEM((ff, width), BF16),
            pltpu.VMEM((width, ff), BF16),
            pltpu.VMEM((width, width), BF16),
            pltpu.SemaphoreType.DMA((3,)),
            pltpu.SemaphoreType.DMA((ff // width + 2,)),
        ],
        compiler_params=params(56),
    )(ctx, tok, cot, vecs, bias_in, w_out, w_in, w_down)


def gather_order(keys, narrow, nd, nb):
    events = []
    for p, (begin, dz, dx) in enumerate(keys):
        for e in range(nb):
            events.append((begin + e * dz, ("z", p, e)))
            if not narrow[p]:
                for mask in range(1, nd):
                    events.append((begin + e * dz + dx * mask.bit_length(), ("x", p, mask, e)))
    events.sort(key=lambda q: q[0])
    return [ev for _, ev in events]


def gather_all(shards, narrow, keys, nd, nb, nc):
    count = len(shards)

    def kernel(*refs):
        mine, full = refs[:count], refs[count:2 * count]
        four, recv, own_sem, block_sem = refs[2 * count:]
        net = Net(nd, nb, nc)
        pieces = [
            Gather(net, mine[p], *blocks_of(full[p]), gather_refs(four, recv, block_sem, p, narrow[p]), narrow[p]) for p in range(count)
        ]
        net.barrier()
        for ev in gather_order(keys, narrow, nd, nb):
            if ev[0] == "z" and ev[2] == 0:
                pieces[ev[1]].own_line()
                pieces[ev[1]].own_spread()
            elif ev[0] == "z":
                pieces[ev[1]].z(ev[2])
            else:
                pieces[ev[1]].x(ev[2], ev[3])
        for piece in pieces:
            own = piece.own(own_sem)
            own.start()
            own.wait()
        for piece in pieces:
            piece.wait_sibling()
        for piece in pieces:
            piece.drain()

    outs = [
        jax.ShapeDtypeStruct(((nb * nc if thin else nd * nb * nc),) + s.shape, s.dtype) for s, thin in zip(shards, narrow)
    ]
    return pl.pallas_call(
        kernel,
        out_shape=outs,
        in_specs=[VMEM] * count,
        out_specs=[HBM] * count,
        scratch_shapes=gather_sems(count, nd, nb) + [pltpu.SemaphoreType.DMA((count, nb))],
        compiler_params=params(56, 0),
    )(*shards)


def attend_forward(tok, w, bias, seg, qlen, width):
    total = tok.shape[0]
    heads = width // HD
    chunk = min(256, qlen)
    while chunk * total > 256 * 4096:
        chunk //= 2
    return pl.pallas_call(
        functools.partial(fwd_kernel, chunk=chunk),
        out_shape=[
            jax.ShapeDtypeStruct((qlen, width), BF16),
            jax.ShapeDtypeStruct((width // 128, total, 256), BF16),
            jax.ShapeDtypeStruct((width // 128, total, 128), BF16),
            jax.ShapeDtypeStruct((heads, qlen, 256), BF16),
            jax.ShapeDtypeStruct((heads, 8, qlen), F32),
            jax.ShapeDtypeStruct((heads // 2, qlen, 128), F32),
        ],
        in_specs=[VMEM] * 4,
        out_specs=[VMEM] * 6,
        scratch_shapes=[pltpu.VMEM((heads, qlen, 128), F32)] * 3,
        compiler_params=params(58),
    )(tok, w, bias, seg)


def pair_bwd_kernel(qaug, kaug, v_scr, lse, exact, gctx, dk, dv, dq, do_m, delta_row, dq_scr):
    step = pl.program_id(1)

    @pl.when(step == 0)
    def _():
        prepare_backward(lambda p: gctx[...], exact, do_m, delta_row)

    def put(k_term, v_term):
        dk[...] = k_term.astype(BF16)
        dv[...] = v_term.astype(BF16)

    bwd_pair(0, qaug, kaug[0], v_scr[0], do_m, lse, delta_row, dq_scr, put, step == 0)

    @pl.when(step == pl.num_programs(1) - 1)
    def _():
        dq[...] = join_dq(dq_scr, 0)


def finish_kernel(tok, dk, dv, tok_mine, dq, w, dtok, dw, dbias, own):
    i, c = pl.program_id(0), lax.axis_index("head")
    blk = lax.axis_index("blk")
    step, width = dk.shape
    qlen = dq.shape[0]

    def cols(part):
        return w[:, pl.ds(pl.multiple_of((part * 2 + c) * width, 128), width)]

    piece, grad_k, grad_v = tok[...], dk[...], dv[...]

    @pl.when(i == 0)
    def _():
        dw[:, 0:width] = dot(tok_mine[...], dq[...], ((0,), (0,)))
        dw[:, width:3 * width] = jnp.zeros((dw.shape[0], 2 * width), F32)
        dbias[0:1, :] = jnp.sum(dq[...].astype(F32), axis=0, keepdims=True)
        dbias[1:2, :] = jnp.zeros((1, width), F32)
        own[...] = dot(dq[...], cols(0), ((1,), (1,)))

    dw[:, width:2 * width] += dot(piece, grad_k, ((0,), (0,)))
    dw[:, 2 * width:3 * width] += dot(piece, grad_v, ((0,), (0,)))
    dbias[1:2, :] += jnp.sum(grad_v.astype(F32), axis=0, keepdims=True)
    grad = dot(grad_k, cols(1), ((1,), (1,))) + dot(grad_v, cols(2), ((1,), (1,)))
    per = qlen // step
    mine = i // per == blk
    at = pl.ds(pl.multiple_of((i % per) * step, step), step)
    dtok[...] = (grad + jnp.where(mine, own[at, :], 0.0)).astype(BF16)


def attend_backward(tok, tok_mine, w, qaug, kaug, v_scr, lse, exact, gctx):
    heads, qlen, _ = qaug.shape
    total, d_model = tok.shape
    width = heads * HD
    kc = min(512, total)
    dk, dv, dq = pl.pallas_call(
        pair_bwd_kernel,
        grid=(heads // 2, total // kc),
        out_shape=[
            jax.ShapeDtypeStruct((total, width), BF16),
            jax.ShapeDtypeStruct((total, width), BF16),
            jax.ShapeDtypeStruct((qlen, width), BF16),
        ],
        in_specs=[
            pl.BlockSpec((2, qlen, 256), lambda p, j: (p, 0, 0)),
            pl.BlockSpec((1, kc, 256), lambda p, j: (p, j, 0)),
            pl.BlockSpec((1, kc, 128), lambda p, j: (p, j, 0)),
            pl.BlockSpec((2, 8, qlen), lambda p, j: (p, 0, 0)),
            pl.BlockSpec((1, qlen, 128), lambda p, j: (p, 0, 0)),
            pl.BlockSpec((qlen, 128), lambda p, j: (0, p)),
        ],
        out_specs=[pl.BlockSpec((kc, 128), lambda p, j: (j, p))] * 2 + [pl.BlockSpec((qlen, 128), lambda p, j: (0, p))],
        scratch_shapes=[
            pltpu.VMEM((2, qlen, 128), BF16),
            pltpu.VMEM((2, 8, qlen), F32),
            pltpu.VMEM((2, 128, qlen), F32),
        ],
        compiler_params=params(56),
    )(qaug, kaug, v_scr, lse, exact, gctx)
    step = min(512, qlen)
    whole = lambda i: (0, 0)
    rows = lambda i: (i, 0)
    return pl.pallas_call(
        finish_kernel,
        grid=(total // step,),
        out_shape=[
            jax.ShapeDtypeStruct((total, d_model), BF16),
            jax.ShapeDtypeStruct((d_model, 3 * width), F32),
            jax.ShapeDtypeStruct((2, width), F32),
        ],
        in_specs=[
            pl.BlockSpec((step, d_model), rows),
            pl.BlockSpec((step, width), rows),
            pl.BlockSpec((step, width), rows),
            pl.BlockSpec((qlen, d_model), whole),
            pl.BlockSpec((qlen, width), whole),
            pl.BlockSpec((d_model, w.shape[1]), whole),
        ],
        out_specs=[
            pl.BlockSpec((step, d_model), rows),
            pl.BlockSpec((d_model, 3 * width), whole),
            pl.BlockSpec((2, width), whole),
        ],
        scratch_shapes=[pltpu.VMEM((qlen, d_model), F32)],
        compiler_params=params(56),
    )(tok, dk, dv, tok_mine, dq, w)


SPACE = (0.25, 1.0, 0.2)


def send_blocks(piece, nb):
    for blk in range(nb):
        piece.send(blk, blk)


def scatter_all(arrays, narrow, joined, small, nd, nb, nc):
    count = len(arrays)
    flat = []
    for a, j in zip(arrays, joined):
        flat += list(a) if j else [a]
    n_in = len(flat) + 1

    def kernel(*refs):
        ins, small_in = list(refs[:n_in - 1]), refs[n_in - 1]
        outs, small_out = refs[n_in:n_in + count], refs[n_in + count]
        rest = list(refs[n_in + count + 1:])
        net = Net(nd, nb, nc)
        s3, sib_sem, x_sem, z_sem, sum_send, sum_recv = rest[-6:]
        value, got = rest[-8:-6]
        bufs = rest[:-8]
        pieces = []
        for p in range(count):
            first = ins.pop(0)
            sib = ins.pop(0) if joined[p] else bufs.pop(0)
            xbuf = None if narrow[p] else bufs.pop(0)
            zbuf = bufs.pop(0)
            sems = [s3.at[p, i] for i in range(3)] + [sib_sem.at[p], x_sem.at[p], z_sem.at[p]]
            if joined[p]:
                parts = lambda at, first=first: [(None, [first.at[at]])]
                place = lambda at, first=first: first.at[at]
                theirs = lambda at, sib=sib: sib.at[at]
                landing = lambda at, first=first: first.at[at, net.c]
            else:
                place = lambda at, first=first: first.at[at * nc + net.c]
                parts = lambda at, place=place, sib=sib: [(None, [place(at), sib.at[at]])]
                theirs = lambda at, first=first: first.at[at * nc + nc - 1 - net.c]
                landing = lambda at, sib=sib: sib.at[at]
            span = lambda k, sib=sib: sib.at[pl.ds(0, k)]
            pieces.append(Scatter(net, parts, place, theirs, landing, span, xbuf, zbuf, outs[p], sems, narrow[p]))
        sums = AllSum(net, value, got, sum_send, sum_recv)
        for piece in pieces:
            piece.clear_edges()
        value[0] = small_in[...]
        net.barrier()
        events = []
        for p, piece in enumerate(pieces):
            t = SPACE[0] * p
            begin = functools.partial(send_blocks, piece, nb) if narrow[p] else piece.start
            events.append((t - 0.4, begin))
            for mask in range(piece.nd - 1, -1, -1):
                for e in range(nb - 1, -1, -1):
                    when = t + SPACE[1] * (piece.levels - mask.bit_length()) + SPACE[2] * (nb - 1 - e)
                    events.append((when, functools.partial(piece.reduce, mask, e)))
        for i, s in enumerate(sums.stages()):
            events.append((0.3 * i, s))
        events.sort(key=lambda q: q[0])
        for _, ev in events:
            ev()
        small_out[...] = value[0]
        for piece in pieces:
            piece.drain()

    outs, scratch = [], []
    for a, thin, j in zip(arrays, narrow, joined):
        full = a[0] if j else a
        block = full.shape[1:]
        outs.append(jax.ShapeDtypeStruct(block, F32))
        n_dp = 1 if thin else nd
        if not j:
            scratch.append(pltpu.VMEM((n_dp * nb,) + block, BF16))
        if not thin:
            scratch.append(pltpu.VMEM(((nd - 1) * nb,) + block, BF16))
        scratch.append(pltpu.VMEM((nb + 1,) + block, BF16))
    levels = nd.bit_length() - 1
    scratch += [pltpu.VMEM((levels + 2,) + small.shape, F32), pltpu.VMEM((levels + nb,) + small.shape, F32)]
    scratch += scatter_sems(count, nd, nb)
    scratch += [pltpu.SemaphoreType.DMA((levels + nb,))] * 2
    outs.append(jax.ShapeDtypeStruct(small.shape, F32))
    return pl.pallas_call(
        kernel,
        out_shape=outs,
        in_specs=[VMEM] * n_in,
        out_specs=[VMEM] * (count + 1),
        scratch_shapes=scratch,
        compiler_params=params(60, 1),
    )(*flat, small)


def hand_out(arrays, small, r, r_ff):
    count = len(arrays)

    def kernel(*refs):
        ins, small_in = refs[:count], refs[count]
        outs, vectors, sems = refs[count + 1:2 * count + 1], refs[2 * count + 1:-1], refs[-1]
        copies = [pltpu.make_async_copy(a, b, sems.at[i]) for i, (a, b) in enumerate(zip(ins, outs))]
        for copy in copies:
            copy.start()
        for i, out in enumerate(vectors):
            out[...] = small_in[i, 0:out.shape[0]]
        for copy in copies:
            copy.wait()

    sizes = [r] * 8 + [r_ff]
    return pl.pallas_call(
        kernel,
        out_shape=[jax.ShapeDtypeStruct(a.shape, a.dtype) for a in arrays] + [jax.ShapeDtypeStruct((s,), F32) for s in sizes],
        in_specs=[VMEM] * (count + 1),
        out_specs=[HBM] * count + [VMEM] * 9,
        scratch_shapes=[pltpu.SemaphoreType.DMA((count,))],
        compiler_params=params(60),
    )(*arrays, small)


def unpack_vectors(small, vecs, bias_in, r, r_ff):
    n = small.shape[0]
    width, ff = vecs.shape[1], bias_in.shape[1]

    def gathered(rows, per, count):
        lane = lax.broadcasted_iota(jnp.int32, (8, 128), 1)
        tiles = [jnp.zeros((8, 128), F32) for _ in range(count // 128)]
        for i in range(n):
            piece = small[i, rows, :].astype(F32)
            shift, tile = per * i % 128, per * i // 128
            if shift:
                piece = pltpu.roll(piece, shift, 1)
            if shift + per <= 128:
                tiles[tile] = tiles[tile] + piece
            else:
                tiles[tile] = tiles[tile] + jnp.where(lane >= shift, piece, 0.0)
                tiles[tile + 1] = tiles[tile + 1] + jnp.where(lane < shift, piece, 0.0)
        return tiles

    for t, tile in enumerate(gathered(slice(0, 8), r, width)):
        vecs[:, t * 128:(t + 1) * 128] = tile
    for t, tile in enumerate(gathered(slice(8, 16), r_ff, ff)):
        bias_in[:, t * 128:(t + 1) * 128] = tile[0:1, :]


def pack_vectors(vectors, bias_in):
    shape = (16,) + vectors[0].shape
    row = lax.broadcasted_iota(jnp.int32, shape, 0)
    few = jnp.zeros(shape, BF16)
    for i, v in enumerate(vectors):
        few = jnp.where(row == i, v[None, :], few)
    return few, jnp.broadcast_to(bias_in[None, :], (16,) + bias_in.shape)


FRONT = {
    "small": (2, 21, ((2, 6, 15, 23), (37, 13, 29, 40), (38, 12, 30, 39), (46, 22, 45, 49))),
    "q": (3, 18, ((3, 10, 14, 25), (32, 17, 26, 41), (31, 19, 28, 43), (44, 33, 42, 51))),
    "t0": (27, 35, ((27, 48, 71, 99),)),
    "t1": (5, 7, ((5, 24, 50, 79),)),
    "o": (0, 83, ((0, 4, 20, 47), (102, 59, 60, 64), (101, 11, 36, 56), (113, 76, 77, 81))),
    "i": (34, 57, ((34, 53, 66, 86), (70, 63, 88, 105), (69, 62, 85, 103), (90, 80, 104, 120))),
    "d": (52, 1, ((52, 73, 94, 107), (9, 93, 112, 121), (8, 92, 111, 119), (16, 108, 122, 125))),
    "work": (54, 55, 58, 61, 65, 67, 68, 72, 74, 75, 78, 82, 84, 87, 89, 91, 95, 96, 97, 98, 100, 106, 109, 110, 114, 115, 116, 117, 118, 123, 124, 126, 127, 128),
}


def front_time(nd, nb, kind, what, e=0):
    if (nd, nb) == (4, 4) and (kind != "work" or e == len(FRONT["work"])):
        row = FRONT[kind]
        if kind == "work":
            return row[what]
        if what == "line":
            return row[0]
        if what == "spread":
            return row[1]
        return row[2][what][e]
    first = ["small", "q", "t0", "t1", "o", "i", "d"].index(kind) * 10 if kind != "work" else 0
    if kind == "work":
        return (40 if what == 0 else 200) + what
    if what in ("line", "spread"):
        return first
    return first + 3 * e + (4 * what.bit_length() if what else 0)


DIRECT = ()


def front(few, many, w_qkv, tok, w_out, w_in, w_down, seg, nd, nb, nc):
    n = nd * nb * nc
    rows, width = tok.shape
    half, qlen, total = width // nc, nc * rows, nb * nc * rows
    heads = half // HD
    pairs = heads // 2
    r, r_ff, ff = w_qkv.shape[0], w_down.shape[0], w_in.shape[1]
    parts = 2
    part = rows // parts
    steps = nb * heads
    chunks = [slice(i, i + width) for i in range(0, ff, width)]

    def kernel(
        few_in, many_in, q_in, tok_in, o_in, i_in, d_in, seg_in,
        ctx2, vecs, lse_out, scale_one,
        q_h, o_h, i_h, d_h, kaug_h, v_h, qaug_h, tok_t_h, act_h, slope_h, exact_h, normed_h, unit_h,
        small_in, small_all, w_v, tok_v, tok_t, kaug, v_scr, qaug, top_scr, sum_scr, o_scr, rest_scr, ctx_loc,
        w_o, w_i, act, slope, bias_in, exact, normed, unit_one,
        four, recv, block_sem, own_sem, load_sem, save_sem, swap_sem,
    ):
        net = Net(nd, nb, nc)
        c = net.c
        small_in[...] = jnp.zeros((16, 128), BF16)
        small_in[:, 0:r] = few_in[...]
        row = lax.broadcasted_iota(jnp.int32, (16, r_ff), 0)
        small_in[:, 0:r_ff] = jnp.where(row == 8, many_in[...], small_in[:, 0:r_ff])
        specs = [("small", small_in, blocks_of(small_all), False), ("q", q_in, rows_of(q_h, r), False)]
        for i in range(parts):
            mine = tok_in.at[pl.ds(i * part, part)]
            specs.append(("t" + str(i), mine, rows_of(tok_v, part, i * part, rows), True))
        specs += [("o", o_in, rows_of(o_h, r), False), ("i", i_in, rows_of(i_h, r), False), ("d", d_in, rows_of(d_h, r_ff), False)]
        piece, own = {}, {}
        for p, (name, mine, (place, span), narrow) in enumerate(specs):
            piece[name] = Gather(net, mine, place, span, gather_refs(four, recv, block_sem, p, narrow), narrow, name in DIRECT)
            own[name] = piece[name].own(own_sem.at[p])
        tokens = ["t" + str(i) for i in range(parts)]
        for name in piece:
            own[name].start()
        net.barrier()
        lanes = pl.ds(pl.multiple_of(c * half, 128), half)

        def whole(name):
            piece[name].wait_sibling()
            own[name].wait()

        def unpack():
            whole("small")
            unpack_vectors(small_all, vecs, bias_in, r, r_ff)

        def load():
            whole("q")
            copies = []
            for k in range(3):
                at = pl.ds(pl.multiple_of((k * nc + c) * half, 128), half)
                copies.append(pltpu.make_async_copy(q_h.at[:, at], w_v.at[:, pl.ds(k * half, half)], load_sem.at[k]))
            for copy in copies:
                copy.start()
            for copy in copies:
                copy.wait()

        def queries():
            for name in tokens:
                own[name].wait()
                piece[name].wait_sibling_block(net.b)
            project_queries(tok_v, w_v[:, 0:half], vecs[0:1, lanes], seg_in, qaug, net.b, qlen)
            for scr, start in ((top_scr, -3e38), (sum_scr, 0.0), (o_scr, 0.0), (rest_scr, 0.0)):
                scr[...] = jnp.full(scr.shape, start, F32)

        saves = [
            pltpu.make_async_copy(src, dst, save_sem.at[i])
            for i, (src, dst) in enumerate(
                [
                    (kaug, kaug_h), (v_scr, v_h), (qaug, qaug_h), (tok_t, tok_t_h),
                    (exact, exact_h), (normed, normed_h), (unit_one, unit_h),
                ]
                + [(a.at[:, at], b.at[:, at]) for a, b in ((act, act_h), (slope, slope_h)) for at in chunks]
            )
        ]

        def turn_tokens():
            tok_t[...] = jnp.transpose(tok_v[...], (1, 0))
            for save in saves[:4]:
                save.start()

        swap = remote(ctx_loc.at[nc - 1 - c], ctx2.at[c], swap_sem.at[0], swap_sem.at[1], net.sibling)
        st = {}

        def finish():
            def put(p, value):
                for g in range(nc):
                    ctx_loc[g, :, p * 128:(p + 1) * 128] = value[g * rows:(g + 1) * rows]

            close_blocks(top_scr, sum_scr, o_scr, rest_scr)
            finish_forward(o_scr, rest_scr, top_scr, put, lse_out, exact)
            swap.start()
            saves[4].start()
            ctx2[c] = ctx_loc[c]

        def fetch(name, src, dst):
            whole(name)
            copy = pltpu.make_async_copy(src, dst, load_sem.at[3])
            copy.start()
            copy.wait()

        def first_norm():
            fetch("o", o_h, w_o)
            swap.wait()
            context = jnp.concatenate([ctx2[g] for g in range(nc)], axis=1)
            resid = tok_in[...].astype(F32) + (dot(context, w_o[...]) + vecs[2:3, :])
            unit, scale = norm_parts(resid)
            value = unit * vecs[3:4, :] + vecs[4:5, :]
            normed[...] = value
            unit_one[...] = unit
            scale_one[...] = jnp.broadcast_to(scale, scale_one.shape)
            saves[5].start()
            saves[6].start()
            st["low"] = value.astype(BF16)

        def expand(i, at):
            if i == 0:
                fetch("i", i_h, w_i)
            pre = dot(st["low"], w_i[:, at]) + bias_in[0:1, at]
            result, grad = gelu_and_slope(pre)
            act[:, at] = result.astype(BF16)
            slope[:, at] = grad
            saves[7 + i].start()
            saves[7 + len(chunks) + i].start()

        order = []
        for name in piece:
            order.append((front_time(nd, nb, name, "line"), piece[name].own_line, None))
            order.append((front_time(nd, nb, name, "spread"), piece[name].own_spread, None))
            for e in range(1, nb):
                order.append((front_time(nd, nb, name, 0, e), functools.partial(piece[name].z, e), None))
            for mask in range(1, 1 if name in tokens else nd):
                for e in range(nb):
                    order.append((front_time(nd, nb, name, mask, e), functools.partial(piece[name].x, mask, e), None))
        work = [unpack, load, queries] + [None] * steps + [turn_tokens, finish, first_norm]
        work += [functools.partial(expand, i, at) for i, at in enumerate(chunks)]
        for i, act_now in enumerate(work):
            order.append((front_time(nd, nb, "work", i, len(work)), act_now, i - 3 if act_now is None else None))
        order.sort(key=lambda q: q[0])
        begin = next(i for i, q in enumerate(order) if q[2] == 0)
        end = next(i for i, q in enumerate(order) if q[2] == steps - 1)
        for _, act_now, _ in order[:begin]:
            act_now()
        beside = {}
        for _, act_now, i in order[begin:end + 1]:
            if act_now is None:
                at_step = i
            else:
                beside.setdefault(at_step, []).append(act_now)

        def attention(e, h, carry):
            blk = net.near(e)
            at = pl.ds(pl.multiple_of(blk * qlen, qlen), qlen)
            attend_block(h, at, qaug, kaug, v_scr, top_scr, sum_scr, o_scr, rest_scr)
            for g in range(heads):
                acts = beside.get(e * heads + g, ())
                if acts:

                    @pl.when(h == g)
                    def _(acts=acts):
                        for act_now in acts:
                            act_now()

            return carry

        for e in range(nb):
            blk = net.near(e)
            if e:
                for name in tokens:
                    piece[name].wait_sibling_block(blk)
            project_keys(blk, qlen, tok_v, w_v[:, half:2 * half], w_v[:, 2 * half:3 * half], vecs[1:2, lanes], seg_in, kaug, v_scr)
            lax.fori_loop(0, heads, functools.partial(attention, e), 0)
        for _, act_now, _ in order[end + 1:]:
            act_now()
        whole("d")
        for name in piece:
            piece[name].drain()
        for save in saves:
            save.wait()

    count = 5 + parts
    vmem = lambda *shape: pltpu.VMEM(shape, BF16)
    wide = pltpu.VMEM((heads, qlen, 128), F32)
    return pl.pallas_call(
        kernel,
        out_shape=[
            jax.ShapeDtypeStruct((nc, rows, half), BF16),
            jax.ShapeDtypeStruct((8, width), F32),
            jax.ShapeDtypeStruct((heads, 8, qlen), F32),
            jax.ShapeDtypeStruct((rows, 128), F32),
            jax.ShapeDtypeStruct((n * r, 3 * width), BF16),
            jax.ShapeDtypeStruct((n * r, width), BF16),
            jax.ShapeDtypeStruct((n * r, ff), BF16),
            jax.ShapeDtypeStruct((n * r_ff, width), BF16),
            jax.ShapeDtypeStruct((pairs, total, 256), BF16),
            jax.ShapeDtypeStruct((pairs, total, 128), BF16),
            jax.ShapeDtypeStruct((heads, qlen, 256), BF16),
            jax.ShapeDtypeStruct((width, total), BF16),
            jax.ShapeDtypeStruct((rows, ff), BF16),
            jax.ShapeDtypeStruct((rows, ff), F32),
            jax.ShapeDtypeStruct((pairs, qlen, 128), F32),
            jax.ShapeDtypeStruct((rows, width), F32),
            jax.ShapeDtypeStruct((rows, width), F32),
        ],
        in_specs=[VMEM] * 8,
        out_specs=[VMEM] * 4 + [HBM] * 13,
        scratch_shapes=[
            vmem(16, 128),
            vmem(n, 16, 128),
            vmem(width, 3 * half),
            vmem(total, width),
            vmem(width, total),
            vmem(pairs, total, 256),
            vmem(pairs, total, 128),
            vmem(heads, qlen, 256),
            wide,
            wide,
            wide,
            wide,
            vmem(nc, rows, half),
            vmem(width, width),
            vmem(width, ff),
            vmem(rows, ff),
            pltpu.VMEM((rows, ff), F32),
            pltpu.VMEM((1, ff), F32),
            pltpu.VMEM((pairs, qlen, 128), F32),
            pltpu.VMEM((rows, width), F32),
            pltpu.VMEM((rows, width), F32),
            pltpu.SemaphoreType.DMA((count, 4)),
            pltpu.SemaphoreType.DMA((count, nd * nb)),
            pltpu.SemaphoreType.DMA((count, nb)),
            pltpu.SemaphoreType.DMA((count,)),
            pltpu.SemaphoreType.DMA((4,)),
            pltpu.SemaphoreType.DMA((7 + 2 * len(chunks),)),
            pltpu.SemaphoreType.DMA((2,)),
        ],
        compiler_params=params(58, 2),
    )(few, many, w_qkv, tok, w_out, w_in, w_down, seg)


BACK = {
    "d": (0, ((64, 49, 47, 42), (50, 25, 21, 18), (26, 15, 14, 13), (27, 11, 8, 7))),
    "i": (0, ((104, 97, 90, 72), (79, 76, 62, 45), (68, 54, 41, 29), (69, 55, 43, 24))),
    "o": (0, ((100, 73, 67, 66), (59, 58, 53, 52), (37, 35, 33, 31), (38, 36, 34, 32))),
    "q": (0, ((103, 99, 95, 94), (98, 93, 88, 85), (91, 86, 82, 81), (92, 87, 83, 80))),
    "t": (0, ((101, 77, 70, 57),)),
    "work": (0, 1, 2, 3, 4, 5, 6, 9, 10, 12, 16, 17, 19, 20, 22, 23, 28, 30, 39, 40, 44, 46, 48, 51, 56, 60, 61, 63, 65, 71, 74, 78, 75, 75.1, 84, 89, 96, 96.1, 102),
}


def back_time(nd, nb, kind, what, e=0):
    if (nd, nb) == (4, 4) and (kind != "work" or e == len(BACK["work"])):
        row = BACK[kind]
        if kind == "work":
            return row[what]
        return row[0] if what == "start" else row[1][what][e]
    if kind == "work":
        return 20 + 10 * what + (100 if what > e - 10 else 0)
    first = {"d": 0, "i": 10, "o": 20, "t": 300, "q": 400}[kind]
    if what == "start":
        return first
    return first + 30 - 5 * what.bit_length() + (nb - 1 - e)


def back(
    ctx, cot, vecs, lse, scale_one, normed, unit_one, exact_in, w_out, w_in, w_down, act_in, slope_in,
    tok_t_in, w_qkv, kaug_in, v_in, qaug_in, nd, nb, nc,
):
    owners = nd * nb
    rows, width = cot.shape
    total = tok_t_in.shape[1]
    ff = w_in.shape[1]
    half, qlen = width // nc, nc * rows
    heads = half // HD
    pairs = heads // 2
    r, r_ff = width // (owners * nc), ff // (owners * nc)
    levels = nd.bit_length() - 1
    names = ["d", "i", "o", "t", "q"]
    chunks = [slice(i, i + width) for i in range(0, ff, width)]
    n_sums = 8 + -(-len(chunks) // 8) * 8

    def kernel(
        ctx_in, cot_in, vecs_in, lse_row, scale_in, normed_h, unit_h, exact_h, wo_h, wi_h, wd_h, act_h, slope_h, tok_t_h, w_h,
        kaug_h, v_h, qaug_h,
        out, g_tok, g_qkv, g_out, g_in, g_down, g_small,
        d_own, i_own, o_own, d_sib, i_sib, o_sib, t_sib, q_sib, d_x, i_x, o_x, q_x, d_z, i_z, o_z, t_z, q_z,
        q_out, resid, gctx, gctx_all, grad_q, normed_in, unit_in, exact, value, got,
        load_sem, swap_sem, s3, sib_sem, x_sem, z_sem, sum_send, sum_recv,
    ):
        net = Net(nd, nb, nc)
        c, other = net.c, nc - 1 - net.c
        piece, held = {}, {}
        for p, (name, own, sib, xbuf, zbuf, result) in enumerate(
            [
                ("d", d_own, d_sib, d_x, d_z, g_down),
                ("i", i_own, i_sib, i_x, i_z, g_in),
                ("o", o_own, o_sib, o_x, o_z, g_out),
                ("t", None, t_sib, None, t_z, g_tok),
                ("q", None, q_sib, q_x, q_z, q_out),
            ]
        ):
            sems = [s3.at[p, i] for i in range(3)] + [sib_sem.at[p], x_sem.at[p], z_sem.at[p]]
            landing = lambda at, sib=sib: sib.at[at]
            span = lambda k, sib=sib: sib.at[pl.ds(0, k)]
            extra = ()
            if name == "t":
                place = lambda at: held["t"].at[at, c]
                parts = lambda at: [(None, [held["t"].at[at, c], t_sib.at[at]])]
                theirs = lambda at: held["t"].at[at, other]
                extra = (resid,)
            elif name == "q":
                place = lambda at: held["q_full"].at[at]
                parts = lambda at: [(c, [held["q"].at[at, c]]), (other, [q_sib.at[at]])]
                theirs = lambda at: held["q"].at[at, other]
            else:
                place = lambda at, own=own: own.at[at]
                parts = lambda at, own=own, sib=sib: [(None, [own.at[at], sib.at[at]])]
                theirs = lambda at, name=name: held[name].at[at]
            piece[name] = Scatter(
                net, parts, place, theirs, landing, span, xbuf, zbuf, result, sems, name == "t", extra, name in "dio", name in "oq"
            )
        whole = AllSum(net, value, got, sum_send, sum_recv)
        swap = remote(gctx.at[other], gctx_all.at[c], swap_sem.at[0], swap_sem.at[1], net.sibling)
        st = {}

        def split(name, at, first, second):
            mine = c == 0
            own = {"d": d_own, "i": i_own, "o": o_own}[name]
            own[at] = jnp.where(mine, first, second).astype(BF16)
            held[name][at] = jnp.where(mine, second, first).astype(BF16)

        def split_rows(name, d, grad, per):
            for a in range(nb):
                at = 2 * a * per
                split(name, d * nb + a, grad[at:at + per], grad[at + per:at + 2 * per])
            piece[name].start_home(d)

        def feed_forward_steps(w_o, w_i, w_d, act, slope, pre_grad, norm_t, ctx_t, d_out, i_out, o_out):
            held.update(d=d_out, i=i_out, o=o_out)
            loads = [
                pltpu.make_async_copy(src, dst, load_sem.at[i])
                for i, (src, dst) in enumerate(
                    [
                        (act_h, act), (wd_h, w_d), (normed_h, normed_in), (slope_h, slope), (wi_h, w_i), (unit_h, unit_in),
                        (wo_h, w_o), (exact_h, exact),
                    ]
                )
            ]
            for load in loads:
                load.start()
            gain_one, bias_down = vecs_in[3:4, :], vecs_in[5:6, :]
            gain_two, shift_two = vecs_in[6:7, :], vecs_in[7:8, :]

            def enter():
                for p in piece.values():
                    p.clear_edges()
                net.barrier()
                ctx_t[...] = jnp.transpose(jnp.concatenate([ctx_in[g] for g in range(nc)], axis=1), (1, 0))
                for load in loads[:3]:
                    load.wait()
                norm_t[...] = jnp.transpose(normed_in[...].astype(BF16), (1, 0))

            def turn():
                unit, scale = norm_parts(normed_in[...] + (dot(act[...], w_d[...]) + bias_down))
                out[...] = (unit * gain_two + shift_two).astype(BF16)
                grad_out = cot_in[...].astype(F32)
                st["two"] = norm_back(grad_out, unit, scale, gain_two)
                st["ffn"] = st["two"].astype(BF16)
                value[0] = jnp.zeros((n_sums, width), F32)
                value[0, 5:6, :] = column_sum(st["ffn"].astype(F32))
                value[0, 6:7, :] = column_sum(grad_out * unit)
                value[0, 7:8, :] = column_sum(grad_out)

            def down(mask):
                d = net.flips(mask)
                lanes = pl.ds(pl.multiple_of(d * (ff // nd), 128), ff // nd)
                split_rows("d", d, dot(act[:, lanes], st["ffn"], ((0,), (0,))), r_ff)

            def pre(i, at):
                if i == 0:
                    loads[3].wait()
                    loads[4].wait()
                grad = (dot(st["ffn"], w_d[at, :], ((1,), (1,))) * slope[:, at]).astype(BF16)
                pre_grad[:, at] = grad
                value[0, 8 + i:9 + i, :] = column_sum(grad.astype(F32))
                st["two"] = st["two"] + dot(grad, w_i[:, at], ((1,), (1,)))

            def norm_one():
                grad = st["two"]
                for load in loads[5:]:
                    load.wait()
                value[0, 3:4, :] = column_sum(grad * unit_in[...])
                value[0, 4:5, :] = column_sum(grad)
                grad = norm_back(grad, unit_in[...], scale_in[:, 0:1], gain_one)
                resid[...] = grad
                st["attn"] = grad.astype(BF16)
                value[0, 2:3, :] = column_sum(st["attn"].astype(F32))
                grad = dot(st["attn"], w_o[...], ((1,), (1,))).astype(BF16)
                for g in range(nc):
                    gctx[g] = grad[:, g * half:(g + 1) * half]
                swap.start()
                gctx_all[c] = gctx[c]

            def weight_in(mask):
                d = net.flips(mask)
                at = pl.ds(pl.multiple_of(d * (width // nd), 8), width // nd)
                split_rows("i", d, dot(norm_t[at, :], pre_grad[...]), r)

            def weight_out():
                for d in range(nd):
                    at = slice(d * (width // nd), (d + 1) * (width // nd))
                    split_rows("o", d, dot(ctx_t[at, :], st["attn"]), r)

            masks = range(nd - 1, -1, -1)
            acts = [enter, turn]
            acts += [functools.partial(down, m) for m in masks]
            acts += [functools.partial(pre, i, at) for i, at in enumerate(chunks)] + [norm_one]
            return acts + [functools.partial(weight_in, m) for m in masks] + [weight_out]

        n_ffn = 4 + len(chunks) + 2 * nd
        steps = nb * pairs
        n_work = n_ffn + 1 + steps + 4 + len(whole.stages())
        order = []
        for name in names:
            p = piece[name]
            for mask in range(p.nd):
                for e in range(nb):
                    order.append((back_time(nd, nb, name, mask, e), functools.partial(p.reduce, mask, e), None))
        for i in range(n_work):
            order.append((back_time(nd, nb, "work", i, n_work), None, i))
        order.sort(key=lambda q: q[0])
        index = [i for i, q in enumerate(order) if q[2] is not None]
        first, last = index[n_ffn + 1], index[n_ffn + steps]

        def run(entries, acts, base):
            for _, act, i in entries:
                (act if i is None else acts[i - base])()

        def feed_forward_scope(*refs):
            run(order[:index[n_ffn - 1] + 1], feed_forward_steps(*refs), 0)
            for name in "dio":
                piece[name].sent()

        def attention_scope(tok_t, w_v, kaug, v_scr, qaug, do_m, delta_row, dq_scr, dkv, t_part, q_part, q_full):
            held.update(t=t_part, q=q_part, q_full=q_full)
            loads = [(qaug_h, qaug)]
            for k in range(3):
                lanes = pl.ds(pl.multiple_of((k * nc + c) * half, 128), half)
                loads.append((w_h.at[:, lanes], w_v.at[:, pl.ds(k * half, half)]))
            loads.append((tok_t_h, tok_t))
            loads = [pltpu.make_async_copy(src, dst, load_sem.at[8 + i]) for i, (src, dst) in enumerate(loads)]

            def block_loads(blk):
                at = pl.ds(pl.multiple_of(blk * qlen, qlen), qlen)
                return [
                    pltpu.make_async_copy(kaug_h.at[:, at], kaug.at[:, at], load_sem.at[13 + blk]),
                    pltpu.make_async_copy(v_h.at[:, at], v_scr.at[:, at], load_sem.at[13 + nb + blk]),
                ]

            loads[0].start()
            for e in range(nb - 1, -1, -1):
                for copy in block_loads(net.near(e)):
                    copy.start()
            for copy in loads[1:]:
                copy.start()

            def prepare():
                swap.wait()
                lane = lambda p: slice(p * 128, (p + 1) * 128)
                prepare_backward(
                    lambda p: jnp.concatenate([gctx_all[g, :, lane(p)] for g in range(nc)], axis=0), exact, do_m, delta_row
                )
                for copy in loads:
                    copy.wait()

            def token_grad(blk):
                at = pl.ds(pl.multiple_of(blk * qlen, qlen), qlen)
                return dot(dkv[at, :], w_v[:, half:3 * half], ((1,), (1,)))

            def put_tokens(blk, grad):
                for g in range(nc):
                    t_part[blk, g] = grad[g * rows:(g + 1) * rows].astype(BF16)
                piece["t"].send(blk, blk)

            def weights():
                grad_q[...] = jnp.concatenate([join_dq(dq_scr, p) for p in range(pairs)], axis=1)
                mine = pl.ds(pl.multiple_of(net.b * qlen, qlen), qlen)
                for k in range(3):
                    if k:
                        grad = dot(tok_t[...], dkv[:, (k - 1) * half:k * half])
                    else:
                        grad = dot(tok_t[:, mine], grad_q[...])
                    for at in range(owners):
                        for g in range(nc):
                            i = at * nc + g
                            q_part[at, g, :, k * half:(k + 1) * half] = grad[i * r:(i + 1) * r].astype(BF16)

            def own_tokens():
                put_tokens(net.b, token_grad(net.b) + dot(grad_q[...], w_v[:, 0:half], ((1,), (1,))))

            def small_sums():
                lanes = pl.ds(pl.multiple_of(c * half, 128), half)
                value[0, 0:1, lanes] = column_sum(grad_q[...].astype(F32))
                value[0, 1:2, lanes] = column_sum(dkv[:, half:2 * half].astype(F32))

            acts = [prepare] + [None] * steps + [weights, piece["q"].start, own_tokens, small_sums] + whole.stages()
            run(order[index[n_ffn - 1] + 1:first], acts, n_ffn)
            beside = {}
            for _, act, i in order[first:last + 1]:
                if i is not None:
                    at_step = i - n_ffn - 1
                else:
                    beside.setdefault(at_step, []).append(act)

            def attention(i, carry):
                pair = i % pairs
                blk = net.near_at(nb - 1 - i // pairs)
                at = pl.ds(pl.multiple_of(blk * qlen, qlen), qlen)

                @pl.when(pair == 0)
                def _():
                    for copy in block_loads(blk):
                        copy.wait()

                def put(dk, dv):
                    dkv[at, pl.ds(pl.multiple_of(pair * 128, 128), 128)] = dk.astype(BF16)
                    dkv[at, pl.ds(pl.multiple_of(half + pair * 128, 128), 128)] = dv.astype(BF16)

                bwd_pair(pair, qaug, kaug[pair, at, :], v_scr[pair, at, :], do_m, lse_row, delta_row, dq_scr, put, i < pairs)

                @pl.when((pair == pairs - 1) & (i < steps - 1))
                def _():
                    put_tokens(blk, token_grad(blk))

                for g, acts in beside.items():

                    @pl.when(i == g)
                    def _(acts=acts):
                        for act in acts:
                            act()

                return carry

            lax.fori_loop(0, steps, attention, 0)
            run(order[last + 1:], acts, n_ffn)
            for k in range(3):
                for g in range(nc):
                    lanes = slice((k * nc + g) * half, (k * nc + g + 1) * half)
                    g_qkv[:, lanes] = q_out[g, :, k * half:(k + 1) * half]
            me = (net.d * nb + net.b) * nc + c
            feature = lax.broadcasted_iota(jnp.int32, (width, 128), 0)
            lane = lax.broadcasted_iota(jnp.int32, (width, 128), 1)
            pick = jnp.where((feature == me * r + lane) & (lane < r), 1.0, 0.0).astype(F32)
            in_row, in_lane = (me * r_ff) // width, (me * r_ff) % width
            pick_in = jnp.where((feature == in_lane + lane) & (lane < r_ff), 1.0, 0.0).astype(F32)
            exactly = dict(precision=lax.Precision.HIGHEST, preferred_element_type=F32)
            g_small[0:8, :] = jnp.dot(value[0, 0:8, :], pick, **exactly)
            found = jnp.dot(value[0, 8:16, :], pick_in, **exactly)
            row = lax.broadcasted_iota(jnp.int32, found.shape, 0)
            g_small[8:16, :] = jnp.broadcast_to(column_sum(jnp.where(row == in_row, found, 0.0)), (8, 128))
            for name in names:
                piece[name].drain()

        pl.run_scoped(feed_forward_scope, *scopes[0])
        pl.run_scoped(attention_scope, *scopes[1])

    block = {"d": (r_ff, width), "i": (r, ff), "o": (r, width), "t": (rows, width)}
    joined = (nc, r, 3 * half)
    vmem = lambda shape, kind=BF16: pltpu.VMEM(shape, kind)
    held_out = [vmem((owners,) + block[k]) for k in "dio"]
    scopes = (
        [
            vmem((width, width)),
            vmem((width, ff)),
            vmem((ff, width)),
            vmem((rows, ff)),
            vmem((rows, ff), F32),
            vmem((rows, ff)),
            vmem((width, rows)),
            vmem((width, rows)),
        ]
        + held_out,
        [
            vmem((width, total)),
            vmem((width, 3 * half)),
            vmem((pairs, total, 256)),
            vmem((pairs, total, 128)),
            vmem((heads, qlen, 256)),
            vmem((heads, qlen, 128)),
            vmem((heads, 8, qlen), F32),
            vmem((heads, 128, qlen), F32),
            vmem((total, 2 * half)),
            vmem((nb, nc, rows, width)),
            vmem((owners,) + joined),
            vmem((owners,) + joined),
        ],
    )
    scratch = [vmem((owners,) + block[k]) for k in "dio"] + [vmem((owners,) + block[k]) for k in "dio"]
    scratch += [vmem((nb,) + block["t"]), vmem((owners, r, 3 * half))]
    scratch += [vmem(((nd - 1) * nb,) + block[k]) for k in "dio"] + [vmem(((nd - 1) * nb,) + joined)]
    scratch += [vmem((nb + 1,) + block[k]) for k in "diot"] + [vmem((nb + 1,) + joined)]
    scratch += [
        vmem(joined, F32),
        vmem((rows, width), F32),
        vmem((nc, rows, half)),
        vmem((nc, rows, half)),
        vmem((qlen, half)),
        vmem((rows, width), F32),
        vmem((rows, width), F32),
        vmem((pairs, qlen, 128), F32),
        vmem((levels + 2, n_sums, width), F32),
        vmem((levels + nb, n_sums, width), F32),
        pltpu.SemaphoreType.DMA((13 + 2 * nb,)),
        pltpu.SemaphoreType.DMA((2,)),
    ]
    scratch += scatter_sems(5, nd, nb) + [pltpu.SemaphoreType.DMA((levels + nb,))] * 2
    return pl.pallas_call(
        kernel,
        out_shape=[
            jax.ShapeDtypeStruct((rows, width), BF16),
            jax.ShapeDtypeStruct((rows, width), F32),
            jax.ShapeDtypeStruct((r, 3 * width), F32),
            jax.ShapeDtypeStruct((r, width), F32),
            jax.ShapeDtypeStruct((r, ff), F32),
            jax.ShapeDtypeStruct((r_ff, width), F32),
            jax.ShapeDtypeStruct((16, 128), F32),
        ],
        in_specs=[VMEM] * 5 + [HBM] * 13,
        out_specs=[VMEM] * 7,
        scratch_shapes=scratch,
        compiler_params=params(62, 3),
    )(
        ctx, cot, vecs, lse, scale_one, normed, unit_one, exact_in, w_out, w_in, w_down, act_in, slope_in,
        tok_t_in, w_qkv, kaug_in, v_in, qaug_in,
    )


def body(
    tokens,
    segment,
    w_qkv,
    bias_query,
    bias_value,
    w_out,
    bias_out,
    gain_attn,
    shift_attn,
    w_in,
    bias_in,
    w_down,
    bias_down,
    gain_ffn,
    shift_ffn,
    cotangent,
):
    nd, nb, nc = lax.axis_size("dp"), lax.axis_size("blk"), lax.axis_size("head")
    n_dev = nd * nb * nc
    d_idx, b_idx, c_idx = lax.axis_index("dp"), lax.axis_index("blk"), lax.axis_index("head")
    me = (d_idx * nb + b_idx) * nc + c_idx
    seqs, rows, width = tokens.shape
    ff = w_in.shape[1]
    half_w = width // nc
    qlen = nc * rows
    r = w_qkv.shape[0]
    r_ff = w_down.shape[0]
    flat_in = tokens.reshape(rows, width)
    cot = cotangent.reshape(rows, width)
    vectors = [bias_query, bias_value, bias_out, gain_attn, shift_attn, bias_down, gain_ffn, shift_ffn]
    if nb * qlen <= 2048 and r % 8 == 0 and ff // width <= 8:
        few, many = pack_vectors(vectors, bias_in)
        (
            ctx2, vecs, lse, scale_one,
            f_qkv, f_out, f_in, f_down, kaug, v_all, qaug, tok_t, act, slope, exact, normed, unit_one,
        ) = front(few, many, w_qkv, flat_in, w_out, w_in, w_down, segment, nd, nb, nc)
        out, g_tok, o_qkv, o_out, o_in, o_down, g_small = back(
            ctx2, cot, vecs, lse, scale_one, normed, unit_one, exact, f_out, f_in, f_down, act, slope,
            tok_t, f_qkv, kaug, v_all, qaug, nd, nb, nc,
        )
        out, g_tok, o_qkv, o_out, o_in, o_down, g_bq, g_bv, g_bo, g_g1, g_s1, g_bd, g_g2, g_s2, g_bin = hand_out(
            [out, g_tok, o_qkv, o_out, o_in, o_down], g_small, r, r_ff
        )
        return (
            out.reshape(seqs, rows, width), g_tok.reshape(seqs, rows, width),
            o_qkv, g_bq, g_bv, o_out, g_bo, g_g1, g_s1, o_in, g_bin, o_down, g_bd, g_g2, g_s2,
        )
    packed = jnp.concatenate(vectors + [bias_in])
    used = packed.shape[0]
    lanes = -(-used // 128) * 128
    packed = jnp.broadcast_to(jnp.pad(packed, (0, lanes - used))[None], (8, lanes))
    n4 = 4
    parts = [flat_in[i * (rows // n4):(i + 1) * (rows // n4)] for i in range(n4)]
    shards = [packed, w_qkv] + parts + [w_out, w_in, w_down]
    narrow = [False, False] + [True] * n4 + [False] * 3
    keys = [(-1, 3, 3), (0, 3, 3), (7, 9, 0), (10, 9, 0), (13, 9, 0), (16, 9, 0), (2, 4, 4), (9, 6, 5), (22, 6, 5)]
    small, g_qkv, t0, t1, t2, t3, g_out, g_in, g_down = gather_all(shards, narrow, keys, nd, nb, nc)
    full_small = small[:, 0, :used]
    vecs = full_small[:, :8 * r].reshape(n_dev, 8, r).transpose(1, 0, 2).reshape(8, width).astype(F32)
    full_bin = full_small[:, 8 * r:].reshape(ff).astype(F32)
    bq, bv, bout, gain_one, shift_one, bdown, gain_two, shift_two = (vecs[i] for i in range(8))
    full_qkv = g_qkv.reshape(width, 3 * width)
    full_wout = g_out.reshape(width, width)
    full_win = g_in.reshape(width, ff)
    full_wdown = g_down.reshape(ff, width)
    tok_all = jnp.stack([t0, t1, t2, t3], axis=1).reshape(nb * qlen, width)
    my_bias = lax.dynamic_slice(vecs, (0, c_idx * half_w), (2, half_w))
    ctx, kaug, v_scr, qaug, lse, exact = attend_forward(tok_all, full_qkv, my_bias, segment, qlen, half_w)
    context_low = ctx.reshape(seqs, qlen, 1, half_w)
    back_tokens = lax.all_to_all(context_low, "head", split_axis=1, concat_axis=2, tiled=True)
    ctx2 = back_tokens.reshape(rows, nc, half_w).transpose(1, 0, 2)
    out, grad_resid_one, gctx2, dw_down, dw_in, dw_out, sums = feed_forward(
        ctx2, flat_in, cot, vecs, full_bin.reshape(1, ff), full_wout, full_win, full_wdown
    )
    output = out.reshape(seqs, rows, width)
    grad_context = gctx2.transpose(1, 0, 2)
    grad_headed = lax.all_to_all(
        grad_context.reshape(seqs, rows, nc, half_w), "head", split_axis=2, concat_axis=1, tiled=True
    )
    gctx = grad_headed.reshape(qlen, half_w)
    tok_mine = lax.dynamic_slice(tok_all, (b_idx * qlen, 0), (qlen, width))
    dtok, dw, dbias = attend_backward(tok_all, tok_mine, full_qkv, qaug, kaug, v_scr, lse, exact, gctx)
    dw = dw.astype(BF16).reshape(nd * nb, nc, r, 3 * half_w)
    ours = lax.dynamic_index_in_dim(dw, c_idx, 1, keepdims=False)
    theirs = lax.dynamic_index_in_dim(dw, 1 - c_idx, 1, keepdims=False)
    joined_full = jnp.stack([ours, ours], axis=1)
    sums = lax.dynamic_update_slice(sums, dbias, (0, c_idx * half_w))
    o_down, o_in, o_out, o_tok, o_qkv, total = scatter_all(
        [
            dw_down.reshape(n_dev, r_ff, width),
            dw_in.reshape(n_dev, r, ff),
            dw_out.reshape(n_dev, r, width),
            dtok.reshape(nb * nc, rows, width),
            (joined_full, theirs),
        ],
        [False, False, False, True, False],
        [False, False, False, False, True],
        sums,
        nd,
        nb,
        nc,
    )
    grad_tokens = (grad_resid_one + o_tok).reshape(seqs, rows, width)
    o_qkv = o_qkv.reshape(2, r, 3, half_w).transpose(1, 2, 0, 3).reshape(r, 3 * width)
    mine = lax.dynamic_slice(total, (0, me * r), (8, r))
    mine_in = lax.dynamic_slice(total[8:8 + ff // width].reshape(ff), (me * r_ff,), (r_ff,))
    g_bq, g_bv, g_bo, g_g1, g_s1, g_bd, g_g2, g_s2 = (mine[i] for i in range(8))
    return (
        output,
        grad_tokens,
        o_qkv,
        g_bq,
        g_bv,
        o_out,
        g_bo,
        g_g1,
        g_s1,
        o_in,
        mine_in,
        o_down,
        g_bd,
        g_g2,
        g_s2,
    )


def solution(mesh):
    weight, vector = P(("dp", "blk", "head"), None), P(("dp", "blk", "head"))
    token = P("dp", ("blk", "head"), None)
    return jax.shard_map(
        body,
        mesh=mesh,
        in_specs=(
            token,
            P("dp", None),
            weight,
            vector,
            vector,
            weight,
            vector,
            vector,
            vector,
            weight,
            vector,
            weight,
            vector,
            vector,
            vector,
            token,
        ),
        out_specs=(
            token,
            token,
            weight,
            vector,
            vector,
            weight,
            vector,
            vector,
            vector,
            weight,
            vector,
            weight,
            vector,
            vector,
            vector,
        ),
        check_vma=False,
    )
```

profile of v0, /device:TPU:0, one launch (start us, length us, event | category | flops | bytes accessed | tf_op | source)
XLA Modules:
  0.0 187.3 jit_solution(12851299323217547680)
XLA Ops:
  0.7 1.5 select_select_fusion.few_in
  2.1 1.2 broadcast_in_dim.69.many_in
  3.4 85.0 %shard_map.271 = (bf16[2,256,384]{2,1,0:T(8,128)(2,1)}, f32[8,768]{1,0:T(8,128)}, f32[6,8,512]{2,1,0:T(8,128)}, f32[256,128]{1,0:T(8,128)}, bf16[768,2304]{1,0:T...) custom-call(bf16[16,24]{1,0:T(8,128)(2,1)} %select_select_fusion.few, ...), custom_call_target="tpu_custom_call" | custom-call | tf_op jit(solution)/shard_map/pallas_call | solution.py:1249
  88.4 95.2 %shard_map.272 = (bf16[256,768]{1,0:T(8,128)(2,1)}, f32[256,768]{1,0:T(8,128)}, f32[24,2304]{1,0:T(8,128)}, f32[24,768]{1,0:T(8,128)}, f32[24,3072]{1,0:T(8,128)}, /*index=5*/f32[96,768]{1,0:T(8,128)}, f32[16,128]{1,0:T(8,128)}) custom-call(bf16[2,256,384]{2,1,0:T(8,128)(2,1)} %get-tuple-element.54.ctx_in, bf16[256,768]{1,0:T(8,128)(2,1)} %bitcast.4, ...), custom_call_target="tpu_custom_call" | custom-call | tf_op jit(solution)/shard_map/pallas_call | solution.py:1682
  183.7 3.4 %shard_map.273 = (bf16[256,768]{1,0:T(8,128)(2,1)}, f32[256,768]{1,0:T(8,128)}, f32[24,2304]{1,0:T(8,128)}, f32[24,768]{1,0:T(8,128)}, f32[24,3072]{1,0:T(8,128)...) custom-call(bf16[256,768]{1,0:T(8,128)(2,1)} %get-tuple-element.71.r, ...), custom_call_target="tpu_custom_call" | custom-call | tf_op jit(solution)/shard_map/pallas_call | solution.py:986
  (4 shorter events, 0.0 us)
where the time goes:
time: 188 us; the launch traced here: 187 us
  Pallas kernels  184 us (98%)
    pallas_call x1, Pallas kernels, back(): pl.pallas_call(kernel, out_shape=[jax.ShapeDtypeStruct((rows, width), BF1...  95.2 us
    pallas_call x1, Pallas kernels, front(): pl.pallas_call(kernel, out_shape=[jax.ShapeDtypeStruct((nc, rows, half),...  85 us

commit v1 on v0

--- a/solution.py
+++ b/solution.py
@@ -1018,24 +1018,15 @@
         bias_in[:, t * 128:(t + 1) * 128] = tile[0:1, :]
 
 
-def pack_vectors(vectors, bias_in):
-    shape = (16,) + vectors[0].shape
-    row = lax.broadcasted_iota(jnp.int32, shape, 0)
-    few = jnp.zeros(shape, BF16)
-    for i, v in enumerate(vectors):
-        few = jnp.where(row == i, v[None, :], few)
-    return few, jnp.broadcast_to(bias_in[None, :], (16,) + bias_in.shape)
-
-
 FRONT = {
-    "small": (2, 21, ((2, 6, 15, 23), (37, 13, 29, 40), (38, 12, 30, 39), (46, 22, 45, 49))),
-    "q": (3, 18, ((3, 10, 14, 25), (32, 17, 26, 41), (31, 19, 28, 43), (44, 33, 42, 51))),
-    "t0": (27, 35, ((27, 48, 71, 99),)),
-    "t1": (5, 7, ((5, 24, 50, 79),)),
-    "o": (0, 83, ((0, 4, 20, 47), (102, 59, 60, 64), (101, 11, 36, 56), (113, 76, 77, 81))),
-    "i": (34, 57, ((34, 53, 66, 86), (70, 63, 88, 105), (69, 62, 85, 103), (90, 80, 104, 120))),
-    "d": (52, 1, ((52, 73, 94, 107), (9, 93, 112, 121), (8, 92, 111, 119), (16, 108, 122, 125))),
-    "work": (54, 55, 58, 61, 65, 67, 68, 72, 74, 75, 78, 82, 84, 87, 89, 91, 95, 96, 97, 98, 100, 106, 109, 110, 114, 115, 116, 117, 118, 123, 124, 126, 127, 128),
+    "small": (2, 22, ((2, 6, 15, 24), (27, 12, 39, 37), (35, 13, 29, 38), (47, 23, 46, 43))),
+    "q": (3, 20, ((3, 10, 14, 25), (30, 16, 28, 40), (34, 17, 44, 45), (41, 32, 42, 50))),
+    "t0": (26, 36, ((26, 54, 71, 99),)),
+    "t1": (4, 8, ((4, 18, 49, 78),)),
+    "o": (0, 89, ((0, 5, 21, 48), (102, 60, 51, 72), (105, 11, 33, 61), (110, 73, 82, 86))),
+    "i": (31, 55, ((31, 53, 64, 84), (69, 62, 91, 103), (70, 65, 81, 100), (88, 83, 104, 121))),
+    "d": (52, 1, ((52, 74, 93, 107), (9, 92, 111, 120), (7, 96, 113, 119), (19, 112, 122, 125))),
+    "work": (56, 57, 58, 59, 63, 66, 67, 68, 75, 76, 77, 79, 80, 85, 87, 90, 94, 95, 97, 98, 101, 106, 108, 109, 114, 115, 116, 117, 118, 123, 124, 126, 127, 128),
 }
 
 
@@ -1060,7 +1051,7 @@
 DIRECT = ()
 
 
-def front(few, many, w_qkv, tok, w_out, w_in, w_down, seg, nd, nb, nc):
+def front(vectors, many, w_qkv, tok, w_out, w_in, w_down, seg, nd, nb, nc):
     n = nd * nb * nc
     rows, width = tok.shape
     half, qlen, total = width // nc, nc * rows, nb * nc * rows
@@ -1073,6 +1064,12 @@
     chunks = [slice(i, i + width) for i in range(0, ff, width)]
 
     def kernel(
+        *refs,
+    ):
+        few_in, many_in = refs[:8], refs[8]
+        inside(few_in, many_in, *refs[9:])
+
+    def inside(
         few_in, many_in, q_in, tok_in, o_in, i_in, d_in, seg_in,
         ctx2, vecs, lse_out, scale_one,
         q_h, o_h, i_h, d_h, kaug_h, v_h, qaug_h, tok_t_h, act_h, slope_h, exact_h, normed_h, unit_h,
@@ -1083,9 +1080,13 @@
         net = Net(nd, nb, nc)
         c = net.c
         small_in[...] = jnp.zeros((16, 128), BF16)
-        small_in[:, 0:r] = few_in[...]
+        few_row = lax.broadcasted_iota(jnp.int32, (16, r), 0)
+        few = jnp.zeros((16, r), BF16)
+        for i, ref in enumerate(few_in):
+            few = jnp.where(few_row == i, jnp.broadcast_to(ref[...], (16, r)), few)
+        small_in[:, 0:r] = few
         row = lax.broadcasted_iota(jnp.int32, (16, r_ff), 0)
-        small_in[:, 0:r_ff] = jnp.where(row == 8, many_in[...], small_in[:, 0:r_ff])
+        small_in[:, 0:r_ff] = jnp.where(row == 8, jnp.broadcast_to(many_in[...], (16, r_ff)), small_in[:, 0:r_ff])
         specs = [("small", small_in, blocks_of(small_all), False), ("q", q_in, rows_of(q_h, r), False)]
         for i in range(parts):
             mine = tok_in.at[pl.ds(i * part, part)]
@@ -1267,7 +1268,7 @@
             jax.ShapeDtypeStruct((rows, width), F32),
             jax.ShapeDtypeStruct((rows, width), F32),
         ],
-        in_specs=[VMEM] * 8,
+        in_specs=[VMEM] * 15,
         out_specs=[VMEM] * 4 + [HBM] * 13,
         scratch_shapes=[
             vmem(16, 128),
@@ -1300,7 +1301,7 @@
             pltpu.SemaphoreType.DMA((2,)),
         ],
         compiler_params=params(58, 2),
-    )(few, many, w_qkv, tok, w_out, w_in, w_down, seg)
+    )(*vectors, many, w_qkv, tok, w_out, w_in, w_down, seg)
 
 
 BACK = {
@@ -1732,11 +1733,10 @@
     cot = cotangent.reshape(rows, width)
     vectors = [bias_query, bias_value, bias_out, gain_attn, shift_attn, bias_down, gain_ffn, shift_ffn]
     if nb * qlen <= 2048 and r % 8 == 0 and ff // width <= 8:
-        few, many = pack_vectors(vectors, bias_in)
         (
             ctx2, vecs, lse, scale_one,
             f_qkv, f_out, f_in, f_down, kaug, v_all, qaug, tok_t, act, slope, exact, normed, unit_one,
-        ) = front(few, many, w_qkv, flat_in, w_out, w_in, w_down, segment, nd, nb, nc)
+        ) = front([v[None, :] for v in vectors], bias_in[None, :], w_qkv, flat_in, w_out, w_in, w_down, segment, nd, nb, nc)
         out, g_tok, o_qkv, o_out, o_in, o_down, g_small = back(
             ctx2, cot, vecs, lse, scale_one, normed, unit_one, exact, f_out, f_in, f_down, act, slope,
             tok_t, f_qkv, kaug, v_all, qaug, nd, nb, nc,

time: 188 us -> 186 us (0.989)
  no operation moved by 1% of the time
where the time goes in v1:
time: 186 us
  Pallas kernels  185 us (99%)
    pallas_call x1, Pallas kernels, back(): pl.pallas_call(kernel, out_shape=[jax.ShapeDtypeStruct((rows, width), BF1...  96.8 us
    pallas_call x1, Pallas kernels, front(): pl.pallas_call(kernel, out_shape=[jax.ShapeDtypeStruct((nc, rows, half),...  84.8 us

profile of v1, /device:TPU:0, one launch (start us, length us, event | category | flops | bytes accessed | tf_op | source)
XLA Modules:
  0.0 185.9 jit_solution(4603006989381743233)
XLA Ops:
  0.7 84.8 %shard_map.271 = (bf16[2,256,384]{2,1,0:T(8,128)(2,1)}, f32[8,768]{1,0:T(8,128)}, f32[6,8,512]{2,1,0:T(8,128)}, f32[256,128]{1,0:T(8,128)}, bf16[768,2304]{1,0:T...) custom-call(bf16[1,24]{1,0:T(2,128)(2,1)} %bitcast.15, ...), custom_call_target="tpu_custom_call" | custom-call | tf_op jit(solution)/shard_map/pallas_call | solution.py:1250
  85.5 96.8 %shard_map.272 = (bf16[256,768]{1,0:T(8,128)(2,1)}, f32[256,768]{1,0:T(8,128)}, f32[24,2304]{1,0:T(8,128)}, f32[24,768]{1,0:T(8,128)}, f32[24,3072]{1,0:T(8,128)}, /*index=5*/f32[96,768]{1,0:T(8,128)}, f32[16,128]{1,0:T(8,128)}) custom-call(bf16[2,256,384]{2,1,0:T(8,128)(2,1)} %get-tuple-element.54.ctx_in, bf16[256,768]{1,0:T(8,128)(2,1)} %bitcast.13, ...), custom_call_target="tpu_custom_call" | custom-call | tf_op jit(solution)/shard_map/pallas_call | solution.py:1683
  182.3 3.4 %shard_map.273 = (bf16[256,768]{1,0:T(8,128)(2,1)}, f32[256,768]{1,0:T(8,128)}, f32[24,2304]{1,0:T(8,128)}, f32[24,768]{1,0:T(8,128)}, f32[24,3072]{1,0:T(8,128)...) custom-call(bf16[256,768]{1,0:T(8,128)(2,1)} %get-tuple-element.71.r, ...), custom_call_target="tpu_custom_call" | custom-call | tf_op jit(solution)/shard_map/pallas_call | solution.py:986

commit v2 on v1

--- a/solution.py
+++ b/solution.py
@@ -57,12 +57,17 @@
         out += [self.across(k) for k in range(self.levels)]
         return out + [self.sibling]
 
+    def greet(self):
+        bar = pltpu.get_barrier_semaphore()
+        for p in self.peers():
+            pl.semaphore_signal(bar, inc=1, device_id=p, device_id_type=MESH)
+
+    def meet(self):
+        pl.semaphore_wait(pltpu.get_barrier_semaphore(), len(self.peers()))
+
     def barrier(self):
-        bar = pltpu.get_barrier_semaphore()
-        ps = self.peers()
-        for p in ps:
-            pl.semaphore_signal(bar, inc=1, device_id=p, device_id_type=MESH)
-        pl.semaphore_wait(bar, len(ps))
+        self.greet()
+        self.meet()
 
 
 def remote(src, dst, send, recv, dev):
@@ -1079,6 +1084,7 @@
     ):
         net = Net(nd, nb, nc)
         c = net.c
+        net.greet()
         small_in[...] = jnp.zeros((16, 128), BF16)
         few_row = lax.broadcasted_iota(jnp.int32, (16, r), 0)
         few = jnp.zeros((16, r), BF16)
@@ -1099,7 +1105,7 @@
         tokens = ["t" + str(i) for i in range(parts)]
         for name in piece:
             own[name].start()
-        net.barrier()
+        net.meet()
         lanes = pl.ds(pl.multiple_of(c * half, 128), half)
 
         def whole(name):
@@ -1420,8 +1426,9 @@
             def enter():
                 for p in piece.values():
                     p.clear_edges()
-                net.barrier()
+                net.greet()
                 ctx_t[...] = jnp.transpose(jnp.concatenate([ctx_in[g] for g in range(nc)], axis=1), (1, 0))
+                net.meet()
                 for load in loads[:3]:
                     load.wait()
                 norm_t[...] = jnp.transpose(normed_in[...].astype(BF16), (1, 0))
@@ -1569,7 +1576,24 @@
                 value[0, 0:1, lanes] = column_sum(grad_q[...].astype(F32))
                 value[0, 1:2, lanes] = column_sum(dkv[:, half:2 * half].astype(F32))
 
-            acts = [prepare] + [None] * steps + [weights, piece["q"].start, own_tokens, small_sums] + whole.stages()
+            stages = whole.stages()
+
+            def pick_small():
+                stages[-1]()
+                me = (net.d * nb + net.b) * nc + c
+                feature = lax.broadcasted_iota(jnp.int32, (width, 128), 0)
+                lane = lax.broadcasted_iota(jnp.int32, (width, 128), 1)
+                pick = jnp.where((feature == me * r + lane) & (lane < r), 1.0, 0.0).astype(F32)
+                in_row, in_lane = (me * r_ff) // width, (me * r_ff) % width
+                pick_in = jnp.where((feature == in_lane + lane) & (lane < r_ff), 1.0, 0.0).astype(F32)
+                exactly = dict(precision=lax.Precision.HIGHEST, preferred_element_type=F32)
+                g_small[0:8, :] = jnp.dot(value[0, 0:8, :], pick, **exactly)
+                found = jnp.dot(value[0, 8:16, :], pick_in, **exactly)
+                row = lax.broadcasted_iota(jnp.int32, found.shape, 0)
+                g_small[8:16, :] = jnp.broadcast_to(column_sum(jnp.where(row == in_row, found, 0.0)), (8, 128))
+
+            acts = [prepare] + [None] * steps + [weights, piece["q"].start, own_tokens, small_sums]
+            acts += stages[:-1] + [pick_small]
             run(order[index[n_ffn - 1] + 1:first], acts, n_ffn)
             beside = {}
             for _, act, i in order[first:last + 1]:
@@ -1613,17 +1637,6 @@
                 for g in range(nc):
                     lanes = slice((k * nc + g) * half, (k * nc + g + 1) * half)
                     g_qkv[:, lanes] = q_out[g, :, k * half:(k + 1) * half]
-            me = (net.d * nb + net.b) * nc + c
-            feature = lax.broadcasted_iota(jnp.int32, (width, 128), 0)
-            lane = lax.broadcasted_iota(jnp.int32, (width, 128), 1)
-            pick = jnp.where((feature == me * r + lane) & (lane < r), 1.0, 0.0).astype(F32)
-            in_row, in_lane = (me * r_ff) // width, (me * r_ff) % width
-            pick_in = jnp.where((feature == in_lane + lane) & (lane < r_ff), 1.0, 0.0).astype(F32)
-            exactly = dict(precision=lax.Precision.HIGHEST, preferred_element_type=F32)
-            g_small[0:8, :] = jnp.dot(value[0, 0:8, :], pick, **exactly)
-            found = jnp.dot(value[0, 8:16, :], pick_in, **exactly)
-            row = lax.broadcasted_iota(jnp.int32, found.shape, 0)
-            g_small[8:16, :] = jnp.broadcast_to(column_sum(jnp.where(row == in_row, found, 0.0)), (8, 128))
             for name in names:
                 piece[name].drain()
 

time: 186 us -> 186 us (level)
  no operation moved by 1% of the time
where the time goes in v2:
time: 186 us; the launch traced here: 185 us
  Pallas kernels  184 us (99%)
    pallas_call x1, Pallas kernels, back(): pl.pallas_call(kernel, out_shape=[jax.ShapeDtypeStruct((rows, width), BF1...  96.7 us
    pallas_call x1, Pallas kernels, front(): pl.pallas_call(kernel, out_shape=[jax.ShapeDtypeStruct((nc, rows, half),...  84.2 us

profile of v2, /device:TPU:0, one launch (start us, length us, event | category | flops | bytes accessed | tf_op | source)
XLA Modules:
  0.0 185.2 jit_solution(14513463216214161927)
XLA Ops:
  0.7 84.2 %shard_map.271 = (bf16[2,256,384]{2,1,0:T(8,128)(2,1)}, f32[8,768]{1,0:T(8,128)}, f32[6,8,512]{2,1,0:T(8,128)}, f32[256,128]{1,0:T(8,128)}, bf16[768,2304]{1,0:T...) custom-call(bf16[1,24]{1,0:T(2,128)(2,1)} %bitcast.15, ...), custom_call_target="tpu_custom_call" | custom-call | tf_op jit(solution)/shard_map/pallas_call | solution.py:1256
  84.9 96.7 %shard_map.272 = (bf16[256,768]{1,0:T(8,128)(2,1)}, f32[256,768]{1,0:T(8,128)}, f32[24,2304]{1,0:T(8,128)}, f32[24,768]{1,0:T(8,128)}, f32[24,3072]{1,0:T(8,128)}, /*index=5*/f32[96,768]{1,0:T(8,128)}, f32[16,128]{1,0:T(8,128)}) custom-call(bf16[2,256,384]{2,1,0:T(8,128)(2,1)} %get-tuple-element.54.ctx_in, bf16[256,768]{1,0:T(8,128)(2,1)} %bitcast.13, ...), custom_call_target="tpu_custom_call" | custom-call | tf_op jit(solution)/shard_map/pallas_call | solution.py:1696
  181.6 3.4 %shard_map.273 = (bf16[256,768]{1,0:T(8,128)(2,1)}, f32[256,768]{1,0:T(8,128)}, f32[24,2304]{1,0:T(8,128)}, f32[24,768]{1,0:T(8,128)}, f32[24,3072]{1,0:T(8,128)...) custom-call(bf16[256,768]{1,0:T(8,128)(2,1)} %get-tuple-element.71.r, ...), custom_call_target="tpu_custom_call" | custom-call | tf_op jit(solution)/shard_map/pallas_call | solution.py:991
